TPU v7x, 512 devices: a whole 4x8x8 slice. The times are simulated.
512 devices in a mesh: elem: 16 (over z, y_hi), span: 32 (over y_lo, x, core).
Axes of the slice: x: 4, y: 8 (y_hi: 2, y_lo: 4; y = y_hi * 4 + y_lo), z: 8, core: 2. Of those that a mesh axis runs over, the one named last changes fastest.
Arguments:
- state: float32 [4, 256, 36864], P(None, 'span', 'elem'), may hold values from -6 to 6
- metric: float32 [2, 1024], P(None, 'elem'), may hold values from -40 to 40, as said below
- neighbour: int32 [1024, 4], P('elem'), may hold values from 0 to 287, as said below
- orient: int32 [1024, 4], P('elem'), may hold values from 0 to 1, as said below
- wall: int32 [1024, 4], P('elem'), may hold values from 0 to 1, as said below
- rim: int32 [2, 256], P(None, 'elem'), may hold values from 0 to 255, as said below
Outputs:
- updated: float32 [4, 256, 36864], P(None, 'span', 'elem')
Inputs may be any that keep to these rules, and one draw needn't show every extreme that they name: neighbour[e, s] is a slot of e's element group's trace pool: e' * 4 + s' for the facing side s' of a local element e' (local index within the group), 256 + r for row r of the lower group's rim, 272 + r for row r of the upper group's rim; on a wall side it is e's own slot. Elements form a channel of 16 rows and 4 columns per group, periodic in x over the groups, in an order drawn per group; elements may be reflected in either reference direction. `orient`: 0 on wall sides. `wall`: 1 exactly on the sides of the first and last rows that face the walls. rim[0, g * 16 + r] is the local slot e * 4 + s of the side of group g's first-column element in row r that faces the lower group; rim[1] likewise for the last column and the upper group. Nonzero; the magnitude of metric[0] is equal along a global column of elements, that of metric[1] along a row; the sign is -1 where the element is reflected in that direction.
All inputs are finite; a program needn't handle non-finite values.
Results may differ from a plain program's by a relative error of at most 0.0003.
Values sent between devices are 32-bit elements; how exact they have to be, the bound alone decides.
A program may use at most 64 MiB of HBM per device.

v0:
```python
import math

import jax
import jax.numpy as jnp
import numpy as np
from jax import lax
from jax.sharding import Mesh
from jax.sharding import PartitionSpec as P

SPAN = ("span_0", "span_1", "span_2")


TIME_STEP = 0.001
VISCOSITY = 0.02
PENALTY = 1.0
HIGHEST = lax.Precision.HIGHEST


def in_blocks(shard, dim, peers):
    before, after = (shard.shape[:dim], shard.shape[dim + 1 :])
    return jnp.moveaxis(shard.reshape(*before, peers, -1, *after), dim, 0)


def joined_along(blocks, dim):
    blocks = jnp.moveaxis(blocks, 0, dim)
    dims = blocks.shape
    return blocks.reshape(*dims[:dim], dims[dim] * dims[dim + 1], *dims[dim + 2 :])


def turned_blocks(blocks, axes, order):
    dims = [lax.axis_size(a) for a in axes]
    blocks = blocks.reshape(*dims, *blocks.shape[1:])
    for k in order:
        blocks = lax.all_to_all(blocks, axes[k], split_axis=k, concat_axis=k, tiled=True)
    return blocks.reshape(-1, *blocks.shape[len(axes) :])


def two_step_exchange(shard, groups, order, split_dim, concat_dim):
    peers = lax.axis_size(groups[0]) * lax.axis_size(groups[1])
    blocks = in_blocks(shard, split_dim, peers)
    return joined_along(turned_blocks(blocks, groups, order), concat_dim)


def from_behind(value, axis, steps):
    count = lax.axis_size(axis)
    pairs = [(source, (source + steps) % count) for source in range(count)]
    return lax.ppermute(value, axis, pairs)


def gll_tables():
    near_point = math.sqrt(1.0 / 3.0 - 2.0 * math.sqrt(7.0) / 21.0)
    far_point = math.sqrt(1.0 / 3.0 + 2.0 * math.sqrt(7.0) / 21.0)
    points = np.array([-1.0, -far_point, -near_point, near_point, far_point, 1.0])
    weights = np.array(
        [
            1.0
            / np.prod([points[column] - points[second] for second in range(6) if second != column])
            for column in range(6)
        ]
    )
    deriv = np.zeros((6, 6))
    for target in range(6):
        for source in range(6):
            if source != target:
                deriv[target, source] = (
                    weights[source] / weights[target] / (points[target] - points[source])
                )
        deriv[target, target] = -np.sum(deriv[target])
    identity = np.eye(6)
    along_x = np.kron(deriv, identity)
    along_y = np.kron(identity, deriv)
    edge_nodes = np.array(
        [
            [offset for offset in range(6)],
            [30 + offset for offset in range(6)],
            [6 * offset for offset in range(6)],
            [6 * offset + 5 for offset in range(6)],
        ]
    ).reshape(-1)
    lifting = np.zeros((36, 24))
    lifting[edge_nodes, np.arange(24)] = 1.0
    return (
        jnp.asarray(along_x, jnp.float32),
        jnp.asarray(along_y, jnp.float32),
        edge_nodes,
        jnp.asarray(lifting, jnp.float32),
    )


def spanwise_basis(count):
    mode_index = jnp.arange(count, dtype=jnp.int32)
    planes = jnp.arange(count, dtype=jnp.int32)
    phase = mode_index[:, None] // 2 * planes[None, :] % count
    phase_angle = phase.astype(jnp.float32) * (2.0 * math.pi / count)
    odd_rows = (mode_index % 2 == 1)[:, None]
    basis_table = jnp.where(odd_rows, jnp.sin(phase_angle), jnp.cos(phase_angle)) * math.sqrt(
        2.0 / count
    )
    alternate = (1 - 2 * (planes % 2)).astype(jnp.float32) / math.sqrt(count)
    constant = jnp.ones((count,), jnp.float32) / math.sqrt(count)
    basis_table = jnp.where(mode_index[:, None] == 0, constant[None, :], basis_table)
    basis_table = jnp.where(mode_index[:, None] == 1, alternate[None, :], basis_table)
    return basis_table


def spanwise_derivative(modal):
    shape_in = modal.shape
    paired = modal.reshape(shape_in[0], shape_in[1] // 2, 2, shape_in[2])
    wavenumber = jnp.arange(shape_in[1] // 2, dtype=jnp.int32).astype(jnp.float32)[None, :, None]
    return jnp.stack([wavenumber * paired[:, :, 1], -wavenumber * paired[:, :, 0]], axis=2).reshape(
        shape_in
    )


def planar_terms(flux_x, flux_y, metric_part):
    along_x, along_y, edge_nodes, lifting = gll_tables()
    scale_x = metric_part[0][:, None]
    scale_y = metric_part[1][:, None]
    grad_x = jnp.einsum("pq,vmeq->vmep", along_x, flux_x, precision=HIGHEST)
    grad_y = jnp.einsum("pq,vmeq->vmep", along_y, flux_y, precision=HIGHEST)
    planar = scale_x * grad_x + scale_y * grad_y
    sign_x = jnp.sign(scale_x)
    sign_y = jnp.sign(scale_y)
    edge_flux = jnp.concatenate(
        [
            -sign_x * flux_x[:, :, :, edge_nodes[0:6]],
            sign_x * flux_x[:, :, :, edge_nodes[6:12]],
            -sign_y * flux_y[:, :, :, edge_nodes[12:18]],
            sign_y * flux_y[:, :, :, edge_nodes[18:24]],
        ],
        axis=3,
    )
    return (planar, edge_flux)


def node_major(flat, num_vars, local_modes, nodes, local_elems):
    return jnp.transpose(flat.reshape(num_vars, local_modes, local_elems, nodes), (0, 1, 3, 2))


def trace_pool(traces):
    shape_in = traces.shape
    return (
        traces.reshape(shape_in[0], shape_in[1], 4, 6, shape_in[3])
        .transpose(0, 1, 3, 4, 2)
        .reshape(shape_in[0], shape_in[1], 6, 4 * shape_in[3])
    )


def own_pools(state_local, normal_flux):
    edge_nodes = gll_tables()[2]
    return (trace_pool(state_local[:, :, edge_nodes, :]), trace_pool(normal_flux))


def update(
    state_local,
    divergence,
    own_q,
    own_flux,
    from_lower,
    from_upper,
    neighbour,
    orient,
    wall,
    metric_local,
    first_mode,
    total_modes,
):
    lifting = gll_tables()[3]
    num_vars, modes_here, num_nodes, count = state_local.shape
    pool_q = jnp.concatenate([own_q, from_lower[0], from_upper[0]], axis=3)
    pool_flux = jnp.concatenate([own_flux, from_lower[1], from_upper[1]], axis=3)
    flat_index = neighbour.reshape(-1)
    other_q = jnp.take(pool_q, flat_index, axis=3)
    other_flux = jnp.take(pool_flux, flat_index, axis=3)
    flipped = orient.reshape(-1) == 1
    other_q = jnp.where(flipped, other_q[:, :, ::-1, :], other_q)
    other_flux = jnp.where(flipped, other_flux[:, :, ::-1, :], other_flux)
    mirror = jnp.array([-1.0, -1.0, -1.0, 1.0], jnp.float32).reshape(4, 1, 1, 1)
    walled = wall.reshape(-1) == 1
    other_q = jnp.where(walled, mirror * own_q, other_q)
    other_flux = jnp.where(walled, mirror * own_flux, other_flux)
    magnitude = (
        jnp.abs(
            jnp.stack([metric_local[0], metric_local[0], metric_local[1], metric_local[1]], axis=1)
        ).reshape(-1)
        * 15.0
    )
    surface_jump = magnitude * (0.5 * (own_flux + other_flux) - 0.5 * PENALTY * (own_q - other_q))
    unpooled = (
        surface_jump.reshape(num_vars, modes_here, 6, count, 4)
        .transpose(0, 1, 4, 2, 3)
        .reshape(num_vars, modes_here, 24, count)
    )
    surface = jnp.einsum("pq,vmqe->vmpe", lifting, unpooled, precision=HIGHEST)
    mode_index = first_mode + jnp.arange(modes_here, dtype=jnp.int32)
    wavenumber = jnp.where(mode_index == 1, total_modes // 2, mode_index // 2).astype(jnp.float32)
    damping = 1.0 + TIME_STEP * VISCOSITY * wavenumber * wavenumber
    return (state_local + TIME_STEP * (surface - divergence)) / damping[None, :, None, None]


def body(state, metric, neighbour, orient, wall, rim):
    num_vars, local_modes, flat_size = state.shape
    num_nodes = 36
    local_elems = flat_size // num_nodes
    span_size = lax.axis_size(SPAN)
    total_modes = local_modes * span_size
    share = local_elems // span_size
    state_nodes = node_major(state, num_vars, local_modes, num_nodes, local_elems)
    planes_in = two_step_exchange(state, (("span_0", "span_1"), "span_2"), (1, 0), 2, 1)
    basis_table = spanwise_basis(total_modes)
    physical = jnp.einsum("mn,vmk->vnk", basis_table, planes_in, precision=HIGHEST)
    metric_part = lax.dynamic_slice_in_dim(metric, lax.axis_index(SPAN) * share, share, axis=1)
    shape_here = (num_vars, total_modes, share, num_nodes)
    planar_div, edge_flux = planar_terms(
        (physical[0:1] * physical).reshape(shape_here),
        (physical[1:2] * physical).reshape(shape_here),
        metric_part,
    )
    volume_fields = jnp.concatenate(
        [planar_div.reshape(num_vars, total_modes, share * num_nodes), physical[2:3] * physical],
        axis=0,
    )
    volume_modal = jnp.einsum("mn,vnk->vmk", basis_table, volume_fields, precision=HIGHEST)
    edge_modal = jnp.einsum(
        "mn,vnk->vmk",
        basis_table,
        edge_flux.reshape(num_vars, total_modes, share * 24),
        precision=HIGHEST,
    )
    combined = volume_modal[0:4] + spanwise_derivative(volume_modal[4:8])
    div_flat, flux_flat = (
        lax.all_to_all(combined, SPAN, split_axis=1, concat_axis=2, tiled=True),
        lax.all_to_all(edge_modal, SPAN, split_axis=1, concat_axis=2, tiled=True),
    )
    divergence = node_major(div_flat, num_vars, local_modes, num_nodes, local_elems)
    normal_flux = node_major(flux_flat, num_vars, local_modes, 24, local_elems)
    own_q, own_flux = own_pools(state_nodes, normal_flux)
    upper_rim = jnp.stack([jnp.take(own_q, rim[1], axis=3), jnp.take(own_flux, rim[1], axis=3)])
    lower_rim = jnp.stack([jnp.take(own_q, rim[0], axis=3), jnp.take(own_flux, rim[0], axis=3)])
    from_lower = from_behind(upper_rim, "elem", 1)
    from_upper = from_behind(lower_rim, "elem", -1)
    first_mode = lax.axis_index(SPAN) * local_modes
    result = update(
        state_nodes,
        divergence,
        own_q,
        own_flux,
        from_lower,
        from_upper,
        neighbour,
        orient,
        wall,
        metric,
        first_mode,
        total_modes,
    )
    return jnp.transpose(result, (0, 1, 3, 2)).reshape(num_vars, local_modes, flat_size)


def solution(mesh):
    torus = Mesh(
        mesh.devices.reshape(mesh.shape["elem"], 4, 4, 2), ("elem", "span_0", "span_1", "span_2")
    )
    in_specs = (
        P(None, SPAN, "elem"),
        P(None, "elem"),
        P("elem", None),
        P("elem", None),
        P("elem", None),
        P(None, "elem"),
    )
    out_specs = P(None, SPAN, "elem")
    return jax.shard_map(body, mesh=torus, in_specs=in_specs, out_specs=out_specs, check_vma=False)
```

profile of v0, /device:TPU:1, one launch (start us, length us, event | category | flops | bytes accessed | tf_op | source)
XLA Modules:
  0.0 166.7 jit_solution(11577555789415481520)
XLA Ops:
  0.0 1.5 reshape.228
  1.8 10.7 %all_to_all.40 = f32[16,2,4,8,72]{4,3,0,2,1:T(8,128)S(1)} all-to-all(f32[16,2,4,8,72]{4,3,0,2,1:T(8,128)S(1)} %copy.269), channel_id=1, replica_groups=mesh['elem'=16,'span_0'=4,'span_1'=4,'span_2'=2] {'span_2'}, dimensions={1} | all-to-all | bytes 589824 | tf_op jit(solution)/shard_map/all_to_all | solution.py:34
  12.5 0.9 copy.270
  13.4 4.2 %all-to-all-start.1 = ((f32[16,2,4,8,72]{4,3,1,2,0:T(8,128)}), f32[16,2,4,8,72]{4,3,1,2,0:T(8,128)}, u32[]{:S(2)}, u32[]{:S(2)}) async-start(f32[16,2,4,8,72]{4,3,1,2,0:T(8,128)} %copy.270), calls=%async_computation.1 | async-start | bytes 1048576 | tf_op jit(solution)/shard_map/all_to_all | solution.py:34
  21.6 1.3 reshape.227
  24.2 1.3 copy.288
  25.5 1.7 %copy.303 = f32[4,8,6,256]{3,1,2,0:T(8,128)} copy(f32[4,8,6,256]{1,3,2,0:T(8,128)S(1)} %bitcast.145) | data formatting | bytes 393216 | tf_op jit(solution)/shard_map/reshape | solution.py:145
  27.3 3.7 %copy.289 = f32[4,8,6,256]{1,0,3,2:T(4,128)} copy(f32[4,8,6,256]{1,3,2,0:T(8,128)S(1)} %bitcast.146) | data formatting | bytes 393216 | tf_op jit(solution)/shard_map/reshape | solution.py:145
  32.7 0.7 eq.73
  33.6 3.2 %gather_fusion.7 = f32[16,4,8,6]{2,1,3,0:T(4,128)} fusion(f32[4,8,6,256]{1,0,3,2:T(4,128)} %copy.289, s32[1024]{0:T(1024)S(1)} %get-tuple-element.41), kind=kCustom, calls=%fused_computation.3.clone | custom fusion | bytes 24640 | tf_op jit(solution)/shard_map/jit(_take)/gather | solution.py:239
  36.8 3.3 %gather_fusion.5 = f32[16,4,8,6]{2,1,3,0:T(4,128)} fusion(f32[4,8,6,256]{1,0,3,2:T(4,128)} %copy.289, s32[1024]{0:T(1024)S(1)} %get-tuple-element.42), kind=kCustom, calls=%fused_computation.clone | custom fusion | bytes 24640 | tf_op jit(solution)/shard_map/jit(_take)/gather | solution.py:238
  40.7 1.1 copy.271
  42.1 1.6 fusion.27
  46.8 1.5 convolution_bitcast_fusion.1
  49.7 1.8 %convolution_bitcast_fusion = f32[8,256,72]{1,2,0:T(8,128)S(1)} fusion(f32[4,256,72]{1,2,0:T(8,128)S(1)} %get-tuple-element.18, f32[4,256,72]{1,2,0:T(8,128)S(1)} %copy.310, s32[256]{0:T(256)S(1)} %copy-done.26, f32[256]{0:T(256)S(1)} %copy-done.25, pred[256]{0:T(512)(128)(4,1)S(1)} %copy-done.29, pred[256]{0:T(512)(128)(4,1)S(1)} %copy-done.27, ...), kind=kOutput, calls=%fused_computation.13 | convolution fusion | flops 454311936 | bytes 1182464 | tf_op jit(solution)/shard_map/mn,vnk->vmk/dot_general | solution.py:223
  51.9 1.2 reshape.361
  53.2 7.8 %all-to-all-start.2 = ((f32[32,1,1536]{2,1,0:T(1,128)}), f32[32,1,1536]{2,1,0:T(1,128)S(1)}, u32[]{:S(2)}, u32[]{:S(2)}) async-start(f32[32,1,1536]{2,1,0:T(1,128)} %reshape.361), calls=%async_computation.2 | async-start | bytes 393216 | tf_op jit(solution)/shard_map/all_to_all | solution.py:233
  62.4 1.0 copy.313
  63.4 7.3 %all-to-all-done.2 = f32[32,1,1536]{2,1,0:T(1,128)S(1)} async-done(((f32[32,1,1536]{2,1,0:T(1,128)}), f32[32,1,1536]{2,1,0:T(1,128)S(1)}, u32[]{:S(2)}, u32[]{:S(2)}) %all-to-all-start.2) | async-done | bytes 196640 | tf_op jit(solution)/shard_map/all_to_all | solution.py:233
  70.6 4.5 %all-to-all-start.3 = ((f32[4,256,72]{2,0,1:T(4,128)}), f32[4,256,72]{2,0,1:T(4,128)}, u32[]{:S(2)}, u32[]{:S(2)}) async-start(f32[4,256,72]{2,0,1:T(4,128)} %copy.313), calls=%async_computation.3 | async-start | bytes 1048576 | tf_op jit(solution)/shard_map/all_to_all | solution.py:232
  75.7 1.1 reduce
  78.0 1.3 copy.281
  79.3 3.7 %copy.293 = f32[4,8,6,256]{1,0,3,2:T(4,128)} copy(f32[4,8,6,256]{1,3,2,0:T(8,128)S(1)} %bitcast.143) | data formatting | bytes 393216 | tf_op jit(solution)/shard_map/reshape | solution.py:145
  83.1 3.2 %gather_fusion.8 = f32[16,4,8,6]{2,1,3,0:T(4,128)} fusion(f32[4,8,6,256]{1,0,3,2:T(4,128)} %copy.293, s32[1024]{0:T(1024)S(1)} %get-tuple-element.41), kind=kCustom, calls=%fused_computation.4.clone | custom fusion | bytes 24640 | tf_op jit(solution)/shard_map/jit(_take)/gather | solution.py:239
  86.3 3.2 %gather_fusion.6 = f32[16,4,8,6]{2,1,3,0:T(4,128)} fusion(f32[4,8,6,256]{1,0,3,2:T(4,128)} %copy.293, s32[1024]{0:T(1024)S(1)} %get-tuple-element.42), kind=kCustom, calls=%fused_computation.2.clone | custom fusion | bytes 24640 | tf_op jit(solution)/shard_map/jit(_take)/gather | solution.py:238
  89.5 1.1 select_bitcast_fusion.5
  90.6 0.8 pad_maximum_fusion.3
  91.5 2.7 %collective-permute-start = (f32[2,4,8,6,16]{2,1,3,4,0:T(4,128)}, f32[2,4,8,6,16]{2,1,3,4,0:T(4,128)}, u32[]{:S(2)}, u32[]{:S(2)}) collective-permute-start(f32[2,4,8,6,16]{2,1,3,4,0:T(4,128)} %pad_maximum_fusion.3), channel_id=1, source_target_pairs={{0,32},{32,64},{64,96},{96,128},{128,160},{160,192},{192,224},{224... | collective-permute-start | bytes 73736 | tf_op jit(solution)/shard_map/ppermute | solution.py:47
  94.2 1.1 select_bitcast_fusion.3
  95.2 0.9 pad_maximum_fusion.4
  96.1 1.7 %copy.297 = f32[4,8,6,256]{3,1,2,0:T(8,128)} copy(f32[4,8,6,256]{1,3,2,0:T(8,128)S(1)} %bitcast.144) | data formatting | bytes 393216 | tf_op jit(solution)/shard_map/reshape | solution.py:145
  97.8 10.4 %collective-permute-start.1 = (f32[2,4,8,6,16]{2,1,3,4,0:T(4,128)}, f32[2,4,8,6,16]{2,1,3,4,0:T(4,128)S(1)}, u32[]{:S(2)}, u32[]{:S(2)}) collective-permute-start(f32[2,4,8,6,16]{2,1,3,4,0:T(4,128)} %pad_maximum_fusion.4), channel_id=1, source_target_pairs={{0,480},{32,0},{64,32},{96,64},{128,96},{160,128},{192,160},{224,1... | collective-permute-start | bytes 73736 | tf_op jit(solution)/shard_map/ppermute | solution.py:47
  108.2 3.9 %collective-permute-done = f32[2,4,8,6,16]{2,1,3,4,0:T(4,128)} collective-permute-done((f32[2,4,8,6,16]{2,1,3,4,0:T(4,128)}, f32[2,4,8,6,16]{2,1,3,4,0:T(4,128)}, u32[]{:S(2)}, u32[]{:S(2)}) %collective-permute-start) | collective-permute-done | bytes 24608 | tf_op jit(solution)/shard_map/ppermute | solution.py:47
  112.2 1.0 slice_bitcast_fusion.1
  113.2 20.3 %collective-permute-done.1 = f32[2,4,8,6,16]{2,1,3,4,0:T(4,128)S(1)} collective-permute-done((f32[2,4,8,6,16]{2,1,3,4,0:T(4,128)}, f32[2,4,8,6,16]{2,1,3,4,0:T(4,128)S(1)}, u32[]{:S(2)}, u32[]{:S(2)}) %collective-permute-start.1) | collective-permute-done | bytes 24608 | tf_op jit(solution)/shard_map/ppermute | solution.py:47
  133.5 3.9 %pad_maximum_fusion.1 = f32[4,8,6,288]{1,0,3,2:T(4,128)} fusion(f32[4,8,6,256]{1,0,3,2:T(4,128)} %copy.289, f32[4,8,6,16]{1,0,2,3:T(4,128)S(1)} %get-tuple-element.13, f32[4,8,6,16]{1,0,2,3:T(4,128)S(1)} %get-tuple-element.15), kind=kLoop, calls=%fused_computation.12 | loop fusion | flops 110592 | bytes 442368 | tf_op jit(solution)/shard_map/concatenate | solution.py:170
  137.4 6.6 %gather_fusion.10 = f32[256,4,8,6]{2,1,3,0:T(4,128)} fusion(f32[4,8,6,288]{1,0,3,2:T(4,128)} %pad_maximum_fusion.1, s32[1024]{0:T(1024)S(1)} %pad_clamp_fusion), kind=kCustom, calls=%fused_computation.5.clone | custom fusion | bytes 394240 | tf_op jit(solution)/shard_map/jit(_take)/gather | solution.py:173
  144.0 3.8 %copy.302 = f32[256,4,8,6]{0,2,3,1:T(8,128)} copy(f32[256,4,8,6]{2,1,3,0:T(4,128)} %gather_fusion.10) | data formatting | bytes 393216 | tf_op jit(solution)/shard_map/jit(_take)/gather | solution.py:173
  147.8 2.2 %pad_maximum_fusion = f32[4,8,6,288]{1,0,3,2:T(4,128)} fusion(f32[4,8,6,256]{1,0,3,2:T(4,128)S(1)} %copy-done, f32[4,8,6,16]{1,0,2,3:T(4,128)S(1)} %get-tuple-element.14, f32[4,8,6,16]{1,0,2,3:T(4,128)S(1)} %get-tuple-element.16), kind=kLoop, calls=%fused_computation.11 | loop fusion | flops 110592 | bytes 442368 | tf_op jit(solution)/shard_map/concatenate | solution.py:171
  150.1 5.1 %gather_fusion.9 = f32[256,4,8,6]{2,1,3,0:T(4,128)S(1)} fusion(f32[4,8,6,288]{1,0,3,2:T(4,128)} %pad_maximum_fusion, s32[1024]{0:T(1024)S(1)} %pad_clamp_fusion), kind=kCustom, calls=%fused_computation.1.clone | custom fusion | bytes 394240 | tf_op jit(solution)/shard_map/jit(_take)/gather | solution.py:174
  155.1 2.0 %copy.296 = f32[256,4,8,6]{0,2,3,1:T(8,128)} copy(f32[256,4,8,6]{2,1,3,0:T(4,128)S(1)} %gather_fusion.9) | data formatting | bytes 393216 | tf_op jit(solution)/shard_map/jit(_take)/gather | solution.py:174
  157.2 1.1 select_bitcast_fusion
  158.3 0.8 fusion.23
  159.1 1.9 %copy.304 = f32[4,8,6,256]{1,3,2,0:T(8,128)S(1)} copy(f32[4,8,6,256]{3,1,2,0:T(8,128)} %fusion.23) | data formatting | bytes 393216 | tf_op jit(solution)/shard_map/mul | solution.py:188
  161.0 1.2 copy.305
  162.2 0.7 fusion.7
  162.9 1.1 copy.350
  165.4 1.3 reshape.247
  (137 shorter events, 17.3 us)
Async XLA Ops:
  0.0 22.9 %copy-start.23 = (s32[24]{0:T(128)S(1)}, s32[24]{0:T(128)}, u32[]{:S(2)}) copy-start(s32[24]{0:T(128)} %constant.160) | copy-start | bytes 292
  0.0 21.6 %copy-start.3 = (f32[4,8,2304]{2,1,0:T(8,128)S(1)}, f32[4,8,2304]{2,1,0:T(8,128)}, u32[]{:S(2)}) copy-start(f32[4,8,2304]{2,1,0:T(8,128)} %param.24) | copy-start | bytes 884740
  0.0 20.9 %copy-start.14 = (s32[64,4]{0,1:T(4,128)S(1)}, s32[64,4]{0,1:T(4,128)}, u32[]{:S(2)}) copy-start(s32[64,4]{0,1:T(4,128)} %param.26) | copy-start | bytes 3076
  13.4 27.3 %all-to-all-start.1 = ((f32[16,2,4,8,72]{4,3,1,2,0:T(8,128)}), f32[16,2,4,8,72]{4,3,1,2,0:T(8,128)}, u32[]{:S(2)}, u32[]{:S(2)}) async-start(f32[16,2,4,8,72]{4,3,1,2,0:T(8,128)} %copy.270), calls=%async_computation.1 | async-start | bytes 1048576 | tf_op jit(solution)/shard_map/all_to_all | solution.py:34
  23.4 0.8 copy-start.1
  27.3 3.8 %copy-start.11 = (f32[2,64]{1,0:T(2,128)S(1)}, f32[2,64]{1,0:T(2,128)}, u32[]{:S(2)}) copy-start(f32[2,64]{1,0:T(2,128)} %param.25) | copy-start | bytes 1540
  27.3 3.8 %copy-start.15 = (s32[64,4]{0,1:T(4,128)S(1)}, s32[64,4]{0,1:T(4,128)}, u32[]{:S(2)}) copy-start(s32[64,4]{0,1:T(4,128)} %param.27) | copy-start | bytes 3076
  27.3 3.9 %copy-start.16 = (s32[64,4]{0,1:T(4,128)S(1)}, s32[64,4]{0,1:T(4,128)}, u32[]{:S(2)}) copy-start(s32[64,4]{0,1:T(4,128)} %param.28) | copy-start | bytes 3076
  27.3 3.9 %copy-start.17 = (s32[2,16]{1,0:T(2,128)S(1)}, s32[2,16]{1,0:T(2,128)}, u32[]{:S(2)}) copy-start(s32[2,16]{1,0:T(2,128)} %param.29) | copy-start | bytes 388
  27.3 4.5 %copy-start.22 = (s32[6]{0:T(128)S(1)}, s32[6]{0:T(128)}, u32[]{:S(2)}) copy-start(s32[6]{0:T(128)} %constant.158) | copy-start | bytes 76
  27.3 4.5 %copy-start.21 = (s32[6]{0:T(128)S(1)}, s32[6]{0:T(128)}, u32[]{:S(2)}) copy-start(s32[6]{0:T(128)} %constant.159) | copy-start | bytes 76
  31.0 11.0 %copy-start.25 = (f32[256]{0:T(256)S(1)}, f32[256]{0:T(256)}, u32[]{:S(2)}) copy-start(f32[256]{0:T(256)} %convert_multiply_fusion) | copy-start | bytes 3076
  31.0 11.0 %copy-start.26 = (s32[256]{0:T(256)S(1)}, s32[256]{0:T(256)}, u32[]{:S(2)}) copy-start(s32[256]{0:T(256)} %and_select_fusion.1) | copy-start | bytes 3076
  31.0 11.0 %copy-start.27 = (pred[256]{0:T(512)(128)(4,1)S(1)}, pred[256]{0:T(512)(128)(4,1)}, u32[]{:S(2)}) copy-start(pred[256]{0:T(512)(128)(4,1)} %get-tuple-element.39) | copy-start | bytes 772
  31.0 11.0 %copy-start.28 = (pred[256]{0:T(512)(128)(4,1)S(1)}, pred[256]{0:T(512)(128)(4,1)}, u32[]{:S(2)}) copy-start(pred[256]{0:T(512)(128)(4,1)} %get-tuple-element.40) | copy-start | bytes 772
  31.0 11.0 %copy-start.29 = (pred[256]{0:T(512)(128)(4,1)S(1)}, pred[256]{0:T(512)(128)(4,1)}, u32[]{:S(2)}) copy-start(pred[256]{0:T(512)(128)(4,1)} %broadcast_compare_fusion.2) | copy-start | bytes 772
  45.2 3.2 %copy-start.8 = (f32[36,36,1,1]{1,0,3,2:T(8,128)S(1)}, f32[36,36,1,1]{1,0,3,2:T(8,128)}, u32[]{:S(2)}) copy-start(f32[36,36,1,1]{1,0,3,2:T(8,128)} %constant.162) | copy-start | bytes 15556
  45.8 3.1 %copy-start.9 = (f32[36,36,1,1]{1,0,3,2:T(8,128)S(1)}, f32[36,36,1,1]{1,0,3,2:T(8,128)}, u32[]{:S(2)}) copy-start(f32[36,36,1,1]{1,0,3,2:T(8,128)} %constant.163) | copy-start | bytes 15556
  49.6 11.4 %copy-start.19 = (f32[128]{0:T(128)S(1)}, f32[128]{0:T(128)}, u32[]{:S(2)}) copy-start(f32[128]{0:T(128)} %fusion.34) | copy-start | bytes 1540
  49.6 11.4 %copy-start.20 = (f32[128]{0:T(128)S(1)}, f32[128]{0:T(128)}, u32[]{:S(2)}) copy-start(f32[128]{0:T(128)} %iota_convert_fusion) | copy-start | bytes 1540
  53.2 17.5 %all-to-all-start.2 = ((f32[32,1,1536]{2,1,0:T(1,128)}), f32[32,1,1536]{2,1,0:T(1,128)S(1)}, u32[]{:S(2)}, u32[]{:S(2)}) async-start(f32[32,1,1536]{2,1,0:T(1,128)} %reshape.361), calls=%async_computation.2 | async-start | bytes 393216 | tf_op jit(solution)/shard_map/all_to_all | solution.py:233
  70.6 92.3 %all-to-all-start.3 = ((f32[4,256,72]{2,0,1:T(4,128)}), f32[4,256,72]{2,0,1:T(4,128)}, u32[]{:S(2)}, u32[]{:S(2)}) async-start(f32[4,256,72]{2,0,1:T(4,128)} %copy.313), calls=%async_computation.3 | async-start | bytes 1048576 | tf_op jit(solution)/shard_map/all_to_all | solution.py:232
  79.3 10.2 %copy-start.7 = (f32[16,4,8,6]{2,1,3,0:T(4,128)S(1)}, f32[16,4,8,6]{2,1,3,0:T(4,128)}, u32[]{:S(2)}) copy-start(f32[16,4,8,6]{2,1,3,0:T(4,128)} %gather_fusion.5) | copy-start | bytes 36868
  79.3 14.8 %copy-start.6 = (f32[16,4,8,6]{2,1,3,0:T(4,128)S(1)}, f32[16,4,8,6]{2,1,3,0:T(4,128)}, u32[]{:S(2)}) copy-start(f32[16,4,8,6]{2,1,3,0:T(4,128)} %gather_fusion.7) | copy-start | bytes 36868
  91.5 20.7 %collective-permute-start = (f32[2,4,8,6,16]{2,1,3,4,0:T(4,128)}, f32[2,4,8,6,16]{2,1,3,4,0:T(4,128)}, u32[]{:S(2)}, u32[]{:S(2)}) collective-permute-start(f32[2,4,8,6,16]{2,1,3,4,0:T(4,128)} %pad_maximum_fusion.3), channel_id=1, source_target_pairs={{0,32},{32,64},{64,96},{96,128},{128,160},{160,192},{192,224},{224... | collective-permute-start | bytes 73736 | tf_op jit(solution)/shard_map/ppermute | solution.py:47
  97.8 35.6 %collective-permute-start.1 = (f32[2,4,8,6,16]{2,1,3,4,0:T(4,128)}, f32[2,4,8,6,16]{2,1,3,4,0:T(4,128)S(1)}, u32[]{:S(2)}, u32[]{:S(2)}) collective-permute-start(f32[2,4,8,6,16]{2,1,3,4,0:T(4,128)} %pad_maximum_fusion.4), channel_id=1, source_target_pairs={{0,480},{32,0},{64,32},{96,64},{128,96},{160,128},{192,160},{224,1... | collective-permute-start | bytes 73736 | tf_op jit(solution)/shard_map/ppermute | solution.py:47
  137.4 10.4 %copy-start = (f32[4,8,6,256]{1,0,3,2:T(4,128)S(1)}, f32[4,8,6,256]{1,0,3,2:T(4,128)}, u32[]{:S(2)}) copy-start(f32[4,8,6,256]{1,0,3,2:T(4,128)} %copy.293) | copy-start | bytes 589828
  150.0 8.2 %copy-start.4 = (f32[4,8,6,256]{3,1,2,0:T(8,128)S(1)}, f32[4,8,6,256]{3,1,2,0:T(8,128)}, u32[]{:S(2)}) copy-start(f32[4,8,6,256]{3,1,2,0:T(8,128)} %copy.303) | copy-start | bytes 589828
  150.0 8.2 %copy-start.5 = (f32[4,8,6,256]{3,1,2,0:T(8,128)S(1)}, f32[4,8,6,256]{3,1,2,0:T(8,128)}, u32[]{:S(2)}) copy-start(f32[4,8,6,256]{3,1,2,0:T(8,128)} %copy.297) | copy-start | bytes 589828
  150.1 8.2 %copy-start.12 = (pred[256]{0:T(512)(128)(4,1)S(1)}, pred[256]{0:T(512)(128)(4,1)}, u32[]{:S(2)}) copy-start(pred[256]{0:T(512)(128)(4,1)} %eq.71) | copy-start | bytes 772
  150.1 8.2 %copy-start.13 = (pred[256]{0:T(512)(128)(4,1)S(1)}, pred[256]{0:T(512)(128)(4,1)}, u32[]{:S(2)}) copy-start(pred[256]{0:T(512)(128)(4,1)} %eq.73) | copy-start | bytes 772
  155.1 3.2 %copy-start.18 = (f32[4]{0:T(128)S(1)}, f32[4]{0:T(128)}, u32[]{:S(2)}) copy-start(f32[4]{0:T(128)} %constant.153.clone) | copy-start | bytes 52
  159.1 3.1 %copy-start.10 = (f32[36,24,1,1]{0,1,3,2:T(8,128)S(1)}, f32[36,24,1,1]{0,1,3,2:T(8,128)}, u32[]{:S(2)}) copy-start(f32[36,24,1,1]{0,1,3,2:T(8,128)} %constant.161) | copy-start | bytes 10372
  162.2 2.6 %copy-start.2 = (f32[4,8,64,36]{2,1,3,0:T(8,128)S(1)}, f32[4,8,64,36]{2,1,3,0:T(8,128)}, u32[]{:S(2)}) copy-start(f32[4,8,64,36]{2,1,3,0:T(8,128)} %copy-done.1) | copy-start | bytes 884740
  162.2 2.6 %copy-start.24 = (f32[8]{0:T(128)S(1)}, f32[8]{0:T(128)}, u32[]{:S(2)}) copy-start(f32[8]{0:T(128)} %fusion.30) | copy-start | bytes 100
where the time goes:
time: 168 us; the launch traced here: 167 us
  local copies, waits for them, and re-layouts  67.9 us (40%)
  waiting for transfers between devices  31.5 us (19%)
  starting transfers between devices  29.6 us (18%)
  other arithmetic  19.7 us (12%)
  blocking collectives  10.7 us (6%)
  matrix products  6.58 us (4%)
    ppermute x2, waiting for transfers between devices, from_behind(): return lax.ppermute(value, axis, pairs)  24.2 us
    ppermute x2, starting transfers between devices, from_behind(): return lax.ppermute(value, axis, pairs)  13.1 us
    reshape x4, local copies, waits for them, and re-layouts, trace_pool(): return traces.reshape(shape_in[0], shape_in[1], 4, 6, shape_in[3]).transp...  10.9 us
    all_to_all x1, blocking collectives, turned_blocks(): lax.all_to_all(blocks, axes[k], split_axis=k, concat_axis=k, tiled=True)  10.7 us
    gather x2, local copies, waits for them, and re-layouts, update(): other_q = jnp.take(pool_q, flat_index, axis=3)  10.4 us
    all_to_all x1, starting transfers between devices, body(): lax.all_to_all(edge_modal, SPAN, split_axis=1, concat_axis=2, tiled=True)  7.84 us
    all_to_all x1, waiting for transfers between devices, body(): lax.all_to_all(edge_modal, SPAN, split_axis=1, concat_axis=2, tiled=True)  7.25 us
    gather x2, local copies, waits for them, and re-layouts, update(): other_flux = jnp.take(pool_flux, flat_index, axis=3)  7.1 us
  transfers between devices with their start and end apart: 5, of which 3 were waited for; matrix products, arithmetic and copies ran while one was open for 45% of the time, Pallas kernels for 0%

commit v1 on v0

v1 whole, which is shorter than its diff:
```python
import functools
import math

import jax
import jax.numpy as jnp
import numpy as np
from jax import lax
from jax.experimental import pallas as pl
from jax.experimental.pallas import tpu as pltpu
from jax.sharding import PartitionSpec as P

TIME_STEP = 0.001
VISCOSITY = 0.02
MESH = pl.DeviceIdType.MESH
F32 = jnp.float32
BF16 = jnp.bfloat16
NODES = 36
PAIR = 72
LANES = 128


def differentiation():
    near = math.sqrt(1.0 / 3.0 - 2.0 * math.sqrt(7.0) / 21.0)
    far = math.sqrt(1.0 / 3.0 + 2.0 * math.sqrt(7.0) / 21.0)
    points = np.array([-1.0, -far, -near, near, far, 1.0])
    weights = np.array(
        [1.0 / np.prod([points[c] - points[s] for s in range(6) if s != c]) for c in range(6)]
    )
    deriv = np.zeros((6, 6))
    for t in range(6):
        for s in range(6):
            if s != t:
                deriv[t, s] = weights[s] / weights[t] / (points[t] - points[s])
        deriv[t, t] = -np.sum(deriv[t])
    return deriv


def split_np(x):
    high = x.astype(jnp.bfloat16)
    low = (x - high.astype(np.float64)).astype(jnp.bfloat16)
    return high, low


def basis_tables(count):
    m = np.arange(count)[:, None]
    n = np.arange(count)[None, :]
    angle = (m // 2 * n % count) * (2.0 * math.pi / count)
    basis = np.where(m % 2 == 1, np.sin(angle), np.cos(angle)) * math.sqrt(2.0 / count)
    basis[0] = 1.0 / math.sqrt(count)
    basis[1] = (1.0 - 2.0 * (np.arange(count) % 2)) / math.sqrt(count)
    minus = np.zeros_like(basis)
    k = np.arange(count // 2)[:, None]
    minus[0::2] = -k * basis[1::2]
    minus[1::2] = k * basis[0::2]
    both = np.concatenate([basis, minus], axis=1)
    return split_np(both)


def node_tables():
    deriv = differentiation()
    ident = np.eye(6)
    two = np.eye(2)
    along_x = np.zeros((PAIR, 192))
    along_y = np.zeros((PAIR, 192))
    lift = np.zeros((PAIR, 192))
    along_x[:, 0:72] = -np.kron(two, np.kron(deriv, ident))
    along_y[:, 72:144] = -np.kron(two, np.kron(ident, deriv))
    for e in range(2):
        for s2 in range(2):
            for j in range(6):
                lane = e * 12 + s2 * 6 + j
                lift[e * 36 + 6 * j + 5 * s2, 144 + lane] = 1.0
                lift[e * 36 + 30 * s2 + j, 168 + lane] = 1.0
    tables = np.stack([along_x, along_y, lift]).astype(np.float32)
    marks = np.zeros((PAIR, 8), np.float32)
    p = np.arange(PAIR) % 36
    marks[:, 0] = 1.0 * (p // 6 == 5) - 1.0 * (p // 6 == 0)
    marks[:, 1] = 1.0 * (p % 6 == 5) - 1.0 * (p % 6 == 0)
    marks[:, 2] = np.abs(marks[:, 0])
    marks[:, 3] = np.abs(marks[:, 1])
    return tables, marks


def lookup_tables(elems, rows):
    spread = np.zeros((elems, elems // 2 * 32))
    marks = np.zeros((8, elems // 2 * 32), np.float32)
    lane = np.arange(elems // 2 * 32)
    r = lane % 32
    used = r < 24
    e = 2 * (lane // 32) + r % 24 // 12
    spread[e[used], lane[used]] = 1.0
    marks[0] = np.where(used, r % 6, 0)
    marks[1] = np.where(used, r // 6 % 2, 0)
    rim_spread = np.zeros((rows, LANES))
    rim_lane = np.arange(6 * rows)
    rim_spread[rim_lane // 6, rim_lane] = 1.0
    marks[2, : 6 * rows] = rim_lane % 6
    return spread.astype(jnp.bfloat16), rim_spread.astype(jnp.bfloat16), marks


def split(x):
    high = x.astype(BF16)
    low = (x - high.astype(F32)).astype(BF16)
    return high, low


def dot3(a, b, dims):
    go = lambda x, y: lax.dot_general(x, y, (dims, ((), ())), preferred_element_type=F32)
    return go(a[0], b[0]) + (go(a[0], b[1]) + go(a[1], b[0]))


def pieces(src, dst, length):
    out = []
    done = 0
    while done < length:
        s, d = src + done, dst + done
        size = min(length - done, LANES - s % LANES, LANES - d % LANES)
        out.append((s // LANES, d // LANES, (d - s) % LANES, d % LANES, d % LANES + size))
        done += size
    return out


class Builder:
    def __init__(self, lane):
        self.lane = lane
        self.tiles = {}
        self.turned = {}

    def add(self, key, load, src, dst, length):
        for st, dt, shift, lo, hi in pieces(src, dst, length):
            name = (key, st, shift)
            if name not in self.turned:
                tile = load(st)
                self.turned[name] = pltpu.roll(tile, shift, 1) if shift else tile
            value = self.turned[name]
            if dt in self.tiles:
                value = jnp.where((self.lane >= lo) & (self.lane < hi), value, self.tiles[dt])
            self.tiles[dt] = value


def kernel(
    groups, span,
    state, metric, neighbour, orient, wall, rim,
    both_high, both_low, node_tab, node_marks, spread, rim_spread, lane_marks,
    out,
    index, flip, others, rim_send, rim_recv, send_a, send_b, recv_a, recv_b,
    fields, rows_r, back_send, back_recv,
    rim_sems, a_sems, b_sems, back_sems,
):
    me = lax.axis_index("span")
    group = lax.axis_index("elem")
    lower = lax.rem(group + groups - 1, groups)
    upper = lax.rem(group + 1, groups)
    elems = metric.shape[1]
    modes = span * 8
    state_tiles = elems * NODES // LANES
    halves = span // 16

    barrier = pltpu.get_barrier_semaphore()

    def greet(k, carry):
        pl.semaphore_signal(
            barrier, 1, device_id=(group, lax.rem(me + k, span)), device_id_type=MESH
        )
        return carry

    pl.semaphore_signal(barrier, 1, device_id=(lower, me), device_id_type=MESH)
    pl.semaphore_signal(barrier, 1, device_id=(upper, me), device_id_type=MESH)
    lax.fori_loop(1, span, greet, 0)

    def bases(slot, reverse):
        side = slot & 3
        vertical = side >= 2
        step = jnp.where(vertical, 6, 1)
        first = jnp.where(vertical, jnp.where(side == 3, 5, 0), jnp.where(side == 1, 30, 0))
        base = NODES * (slot >> 2) + first
        return base, step

    def spread_over(values, matrix, dims):
        high = (values >> 6).astype(F32).astype(BF16)
        low = (values & 63).astype(F32).astype(BF16)
        go = lambda x: lax.dot_general(x, matrix, (dims, ((), ())), preferred_element_type=F32)
        return (go(high) * 64.0 + go(low)).astype(jnp.int32)

    rim_base, rim_step = bases(rim[...], None)
    natural = ((1,), (0,))
    node_r = lane_marks[2:3, 0:LANES].astype(jnp.int32)
    rim_index = spread_over(rim_base, rim_spread[...], natural) + node_r * spread_over(
        rim_step, rim_spread[...], natural
    )

    slot = neighbour[...]
    turn = orient[...]
    remote = slot >= 4 * elems
    base, step = bases(slot, None)
    row = slot - 4 * elems
    base = jnp.where(remote, state_tiles * LANES + LANES * (row >> 4) + 6 * (row & 15), base)
    step = jnp.where(remote, 1, step)
    base = jnp.where(turn == 1, base + 5 * step, base)
    step = jnp.where(turn == 1, -step, step)
    over = ((0,), (0,))
    matrix = spread[...]
    base_l = spread_over(base, matrix, over)
    step_l = spread_over(step + 64, matrix, over) - 64
    wall_l = spread_over(wall[...], matrix, over)
    node_l = lane_marks[0:1, :].astype(jnp.int32)
    second = lane_marks[1:2, :] > 0.5
    used = spread_over(jnp.ones_like(slot), matrix, over)[0:1] > 0
    for axis in range(2):
        pick = lambda x: jnp.where(second, x[2 * axis + 1 : 2 * axis + 2], x[2 * axis : 2 * axis + 1])
        lanes_at = jnp.where(used, pick(base_l) + pick(step_l) * node_l, 0)
        walls = 1.0 - 2.0 * pick(wall_l).astype(F32)
        for t in range(index.shape[1]):
            cut = slice(t * LANES, (t + 1) * LANES)
            index[axis, t] = jnp.broadcast_to(lanes_at[:, cut], (8, LANES))
            flip[axis, t] = jnp.broadcast_to(walls[:, cut], (8, LANES))

    def gather(at, start, tiles):
        low = at & (LANES - 1)
        high = at >> 7
        totals = list(start)
        for k in tiles:
            here = high == k
            for v in range(4):
                tile = (
                    state[v, :, k * LANES : (k + 1) * LANES]
                    if k < state_tiles
                    else rim_recv[k - state_tiles, v]
                )
                got = jnp.take_along_axis(tile, low, axis=1, mode="promise_in_bounds")
                totals[v] = jnp.where(here, got, totals[v])
        return totals

    zero = [jnp.zeros((8, LANES), F32)] * 4
    for way in range(2):
        at = jnp.broadcast_to(rim_index[way : way + 1], (8, LANES))
        got = gather(at, zero, range(state_tiles))
        for v in range(4):
            rim_send[way, v] = got[v]

    pl.semaphore_wait(barrier, span + 1)

    rim_copies = [
        pltpu.make_async_remote_copy(
            rim_send.at[way], rim_recv.at[1 - way], rim_sems.at[way], rim_sems.at[3 - way],
            device_id=(to, me), device_id_type=MESH,
        )
        for way, to in ((0, lower), (1, upper))
    ]
    for copy in rim_copies:
        copy.start()

    lane = lax.broadcasted_iota(jnp.int32, (8, LANES), 1)

    def gather_axis(axis, tiles, first):
        def one(t, carry):
            at = index[axis, t]
            start = zero if first else [others[axis, v, t] for v in range(4)]
            got = gather(at, start, tiles)
            for v in range(4):
                others[axis, v, t] = got[v]
            return carry

        lax.fori_loop(0, index.shape[1], one, 0)

    gather_axis(1, range(state_tiles), True)

    def reflected(axis, v, t):
        tile = others[axis, v, t]
        return tile * flip[axis, t] if v < 3 else tile

    for d in range(span):
        b = Builder(lane)
        for v in range(4):
            b.add(
                ("own", v),
                lambda k, v=v: state[v, :, k * LANES : (k + 1) * LANES],
                PAIR * d, 96 * v, PAIR,
            )
            b.add(("other", v), lambda k, v=v: reflected(1, v, k), 32 * d, 96 * v + PAIR, 24)
        for k in range(3):
            send_a[d, :, k * LANES : (k + 1) * LANES] = b.tiles[k]

    def exchange(src, dst, sems):
        def one(k, carry):
            to = lax.rem(me + k, span)
            pltpu.make_async_remote_copy(
                src(to), dst(me), sems.at[0], sems.at[1],
                device_id=(group, to), device_id_type=MESH,
            ).start()
            return carry

        lax.fori_loop(1, span, one, 0)
        pltpu.make_async_copy(src(me), dst(me), sems.at[1]).start()

    mode_rows = lambda who: pl.ds(pl.multiple_of(8 * who, 8), 8)
    exchange(lambda to: send_a.at[to], lambda who: recv_a.at[mode_rows(who), :], a_sems)

    gather_axis(0, range(state_tiles), True)
    for copy in rim_copies:
        copy.wait()
    gather_axis(0, range(state_tiles, state_tiles + 2), False)
    for d in range(span):
        b = Builder(lane)
        for v in range(4):
            b.add(("other", v), lambda k, v=v: reflected(0, v, k), 32 * d, 24 * v, 24)
        send_b[d] = b.tiles[0]
    exchange(lambda to: send_b.at[to], lambda who: recv_b.at[mode_rows(who), :], b_sems)

    at = lax.broadcasted_iota(jnp.int32, (2, elems), 1)
    scale = metric[...]
    first = jnp.sum(jnp.where(at == 2 * me, scale, 0.0), axis=1, keepdims=True)
    last = jnp.sum(jnp.where(at == 2 * me + 1, scale, 0.0), axis=1, keepdims=True)

    def per_row(rows, which):
        e = lax.broadcasted_iota(jnp.int32, (rows, 1), 0)
        return jnp.where(e < rows // 2, first[which : which + 1], last[which : which + 1])

    rx, ry = per_row(PAIR, 0), per_row(PAIR, 1)
    marks = node_marks[...]
    coef_u = 7.5 * rx * marks[:, 0:1]
    coef_v = 7.5 * ry * marks[:, 1:2]
    coef_c = 7.5 * (jnp.abs(rx) * marks[:, 2:3] + jnp.abs(ry) * marks[:, 3:4])
    operator = split(rx * node_tab[0] + ry * node_tab[1] + node_tab[2])
    side = lax.broadcasted_iota(jnp.int32, (24, 1), 0)
    low_side = (side < 6) | ((side >= 12) & (side < 18))
    toward = jnp.where(low_side, 7.5, -7.5)
    ox, oy = per_row(24, 0), per_row(24, 1)

    over0 = ((0,), (0,))
    pltpu.make_async_copy(recv_a, recv_a, a_sems.at[1]).wait()
    basis = (both_high[:, 0:modes], both_low[:, 0:modes])
    planes_a = dot3(split(recv_a[...]), basis, over0)
    own = [planes_a[96 * v : 96 * v + PAIR] for v in range(4)]
    facing_y = [planes_a[96 * v + PAIR : 96 * v + 96] for v in range(4)]
    own_coef = coef_u * own[0] + coef_v * own[1] - coef_c
    facing_y_coef = (toward * oy) * facing_y[1] + 7.5 * jnp.abs(oy)
    for v in range(4):
        fields[v, 0:72] = own[0] * own[v]
        fields[v, 72:144] = own[1] * own[v]
        fields[v, 144:168] = facing_y_coef * facing_y[v]
        rows_r[72 * v : 72 * v + 72, modes : 2 * modes] = own[2] * own[v]
        rows_r[72 * v : 72 * v + 72, 0:modes] = own_coef * own[v]

    pltpu.make_async_copy(recv_b, recv_b, b_sems.at[1]).wait()
    planes_b = dot3(split(recv_b[...]), basis, over0)
    facing_x = [planes_b[24 * v : 24 * v + 24] for v in range(4)]
    facing_x_coef = (toward * ox) * facing_x[0] + 7.5 * jnp.abs(ox)
    for v in range(4):
        fields[v, 168:192] = facing_x_coef * facing_x[v]
        rows_r[72 * v : 72 * v + 72, 0:modes] += dot3(operator, split(fields[v]), ((1,), (0,)))

    back_send[:, 0:288] = dot3(
        (both_high[...], both_low[...]), split(rows_r[...]), ((1,), (1,))
    )
    exchange(lambda to: back_send.at[mode_rows(to), :], lambda who: back_recv.at[who], back_sems)
    pltpu.make_async_copy(back_recv, back_recv, back_sems.at[1]).wait()

    mode = 8 * me + lax.broadcasted_iota(jnp.int32, (8, LANES), 0)
    k = jnp.where(mode == 1, modes // 2, mode >> 1).astype(F32)
    shrink = 1.0 / (1.0 + TIME_STEP * VISCOSITY * k * k)
    builders = [Builder(lane) for _ in range(4)]
    for d in range(span):
        for v in range(4):
            builders[v].add(
                d, lambda t, d=d: back_recv[d, :, t * LANES : (t + 1) * LANES],
                PAIR * v, PAIR * d, PAIR,
            )
    for v in range(4):
        for t in range(state_tiles):
            cut = slice(t * LANES, (t + 1) * LANES)
            out[v, :, cut] = (state[v, :, cut] + TIME_STEP * builders[v].tiles[t]) * shrink

    pltpu.make_async_copy(send_a.at[0 : span - 1], send_a.at[0 : span - 1], a_sems.at[0]).wait()
    pltpu.make_async_copy(send_b.at[0 : span - 1], send_b.at[0 : span - 1], b_sems.at[0]).wait()
    sent = back_send.at[0 : 8 * (span - 1), :]
    pltpu.make_async_copy(sent, sent, back_sems.at[0]).wait()


def body(groups, span, state, metric, neighbour, orient, wall, rim):
    elems = metric.shape[1]
    modes = span * 8
    tables, marks = node_tables()
    spread, rim_spread, lane_marks = lookup_tables(elems, rim.shape[1])
    both_high, both_low = basis_tables(modes)
    constants = [both_high, both_low, tables, marks, spread, rim_spread, lane_marks]
    constants = [jnp.asarray(c) for c in constants]
    vmem = pl.BlockSpec(memory_space=pltpu.VMEM)
    gathered = elems // 2 * 32 // LANES
    scratch = [
        pltpu.VMEM((2, gathered, 8, LANES), jnp.int32),
        pltpu.VMEM((2, gathered, 8, LANES), F32),
        pltpu.VMEM((2, 4, gathered, 8, LANES), F32),
        pltpu.VMEM((2, 4, 8, LANES), F32),
        pltpu.VMEM((2, 4, 8, LANES), F32),
        pltpu.VMEM((span, 8, 384), F32),
        pltpu.VMEM((span, 8, LANES), F32),
        pltpu.VMEM((modes, 384), F32),
        pltpu.VMEM((modes, LANES), F32),
        pltpu.VMEM((4, 192, modes), F32),
        pltpu.VMEM((288, 2 * modes), F32),
        pltpu.VMEM((modes, 384), F32),
        pltpu.VMEM((span, 8, 384), F32),
        pltpu.SemaphoreType.DMA((4,)),
        pltpu.SemaphoreType.DMA((2,)),
        pltpu.SemaphoreType.DMA((2,)),
        pltpu.SemaphoreType.DMA((2,)),
    ]
    return pl.pallas_call(
        functools.partial(kernel, groups, span),
        out_shape=jax.ShapeDtypeStruct(state.shape, F32),
        in_specs=[vmem] * 13,
        out_specs=vmem,
        scratch_shapes=scratch,
        compiler_params=pltpu.CompilerParams(
            collective_id=0, has_side_effects=True, vmem_limit_bytes=40 << 20
        ),
        name="section",
    )(state, metric, neighbour, orient, wall, rim, *constants)


def solution(mesh):
    specs = (
        P(None, "span", "elem"), P(None, "elem"), P("elem", None),
        P("elem", None), P("elem", None), P(None, "elem"),
    )
    return jax.shard_map(
        functools.partial(body, mesh.shape["elem"], mesh.shape["span"]),
        mesh=mesh, in_specs=specs, out_specs=P(None, "span", "elem"), check_vma=False,
    )
```

time: 168 us -> 50.2 us (0.30)
  the two profiles are of different devices: /device:TPU:1 before, /device:TPU:15 now
where the time goes in v1:
time: 50.2 us; the launch traced here: 49.9 us
  Pallas kernels  42.8 us (85%)
  local copies, waits for them, and re-layouts  6.99 us (14%)
    pallas_call x1, Pallas kernels, body(): pl.pallas_call(functools.partial(kernel, groups, span), out_shape=jax.Sha...  42.8 us
    unnamed x28, local copies, waits for them, and re-layouts  6.99 us

profile of v1, /device:TPU:15, one launch (start us, length us, event | category | flops | bytes accessed | tf_op | source)
XLA Modules:
  0.0 49.9 jit_solution(17962944283875523087)
XLA Ops:
  0.0 0.0 copy-start.10
  0.0 0.0 copy-start.11
  0.0 0.0 copy-start.7
  0.0 0.0 copy-start.8
  0.0 0.0 copy-start.9
  0.0 0.8 %copy.14.neighbour = s32[64,4]{1,0:T(8,128)S(1)} copy(s32[64,4]{0,1:T(4,128)} %param.15) | data formatting | bytes 2048 | tf_op args[2]
  0.8 0.0 copy-done.10
  0.9 0.0 copy-start.5
  0.9 0.0 copy-start.6
  0.9 0.1 copy.15.orient
  1.0 0.0 copy-done.11
  1.0 0.1 copy.16.wall
  1.1 0.0 copy-done.7
  1.1 0.0 copy-done.8
  1.1 0.0 copy-done.9
  1.1 0.5 %copy-done.5 = f32[72,8]{1,0:T(8,128)S(1)} copy-done((f32[72,8]{1,0:T(8,128)S(1)}, f32[72,8]{1,0:T(8,128)}, u32[]{:S(2)}) %copy-start.5) | copy-done | bytes 2328
  1.6 0.0 copy-done.6
  1.6 0.0 copy-start
  1.6 1.0 %copy-done = f32[4,8,2304]{2,1,0:T(8,128)S(1)} copy-done((f32[4,8,2304]{2,1,0:T(8,128)S(1)}, f32[4,8,2304]{2,1,0:T(8,128)}, u32[]{:S(2)}) %copy-start) | copy-done | bytes 294936
  2.6 0.0 copy-start.1
  2.6 0.9 %copy-done.1 = bf16[256,512]{1,0:T(8,128)(2,1)S(1)} copy-done((bf16[256,512]{1,0:T(8,128)(2,1)S(1)}, bf16[256,512]{1,0:T(8,128)(2,1)}, u32[]{:S(2)}) %copy-start.1) | copy-done | bytes 262168
  3.5 0.0 copy-start.2
  3.5 0.9 %copy-done.2 = bf16[256,512]{1,0:T(8,128)(2,1)S(1)} copy-done((bf16[256,512]{1,0:T(8,128)(2,1)S(1)}, bf16[256,512]{1,0:T(8,128)(2,1)}, u32[]{:S(2)}) %copy-start.2) | copy-done | bytes 262168
  4.5 0.0 copy-start.3
  4.5 0.9 %copy-done.3 = f32[3,72,192]{2,1,0:T(8,128)S(1)} copy-done((f32[3,72,192]{2,1,0:T(8,128)S(1)}, f32[3,72,192]{2,1,0:T(8,128)}, u32[]{:S(2)}) %copy-start.3) | copy-done | bytes 165912
  5.4 0.0 copy-start.4
  5.4 0.9 %copy-done.4 = bf16[64,1024]{1,0:T(8,128)(2,1)S(1)} copy-done((bf16[64,1024]{1,0:T(8,128)(2,1)S(1)}, bf16[64,1024]{1,0:T(8,128)(2,1)}, u32[]{:S(2)}) %copy-start.4) | copy-done | bytes 131096
  6.3 42.8 %section.1 = f32[4,8,2304]{2,1,0:T(8,128)S(1)} custom-call(f32[4,8,2304]{2,1,0:T(8,128)S(1)} %copy-done, f32[2,64]{1,0:T(2,128)S(1)} %copy-done.8, s32[64,4]{1,0:T(8,128)S(1)} %copy.14.neighbour, s32[64,4]{1,0:T(8,128)S(1)} %copy.15.orient, s32[64,4]{1,0:T(8,128)S(1)} %copy.16.wall, s32[2,16]{1,0:T(2,128)S(1)} %copy-done.9, bf16[256,512]{1,0:T(8,128)(2,1)S(1)} %copy-done.2, ...), custom_call_target="tpu_custom_call" | custom-call | tf_op jit(solution)/shard_map/section/pallas_call | solution.py:409
  49.1 0.7 %copy.18 = f32[4,8,2304]{2,1,0:T(8,128)} copy(f32[4,8,2304]{2,1,0:T(8,128)S(1)} %section.1) | data formatting | bytes 589824
Async XLA Ops:
  0.0 0.9 %copy-start.10 = (s32[64,4]{0,1:T(4,128)S(1)}, s32[64,4]{0,1:T(4,128)}, u32[]{:S(2)}) copy-start(s32[64,4]{0,1:T(4,128)} %param.16) | copy-start | bytes 3076
  0.0 1.0 %copy-start.11 = (s32[64,4]{0,1:T(4,128)S(1)}, s32[64,4]{0,1:T(4,128)}, u32[]{:S(2)}) copy-start(s32[64,4]{0,1:T(4,128)} %param.17) | copy-start | bytes 3076
  0.0 1.1 %copy-start.7 = (bf16[16,128]{1,0:T(8,128)(2,1)S(1)}, bf16[16,128]{1,0:T(8,128)(2,1)}, u32[]{:S(2)}) copy-start(bf16[16,128]{1,0:T(8,128)(2,1)} %constant.19.clone.rim_spread) | copy-start | bytes 12292
  0.0 1.1 %copy-start.8 = (f32[2,64]{1,0:T(2,128)S(1)}, f32[2,64]{1,0:T(2,128)}, u32[]{:S(2)}) copy-start(f32[2,64]{1,0:T(2,128)} %metric.1) | copy-start | bytes 1540
  0.0 1.1 %copy-start.9 = (s32[2,16]{1,0:T(2,128)S(1)}, s32[2,16]{1,0:T(2,128)}, u32[]{:S(2)}) copy-start(s32[2,16]{1,0:T(2,128)} %rim.1) | copy-start | bytes 388
  0.9 0.8 %copy-start.5 = (f32[72,8]{1,0:T(8,128)S(1)}, f32[72,8]{1,0:T(8,128)}, u32[]{:S(2)}) copy-start(f32[72,8]{1,0:T(8,128)} %constant.17.clone.node_marks) | copy-start | bytes 6916
  0.9 0.8 %copy-start.6 = (f32[8,1024]{1,0:T(8,128)S(1)}, f32[8,1024]{1,0:T(8,128)}, u32[]{:S(2)}) copy-start(f32[8,1024]{1,0:T(8,128)} %constant.20.clone.lane_marks) | copy-start | bytes 98308
  1.6 1.0 %copy-start = (f32[4,8,2304]{2,1,0:T(8,128)S(1)}, f32[4,8,2304]{2,1,0:T(8,128)}, u32[]{:S(2)}) copy-start(f32[4,8,2304]{2,1,0:T(8,128)} %state.1) | copy-start | bytes 884740
  2.6 0.9 %copy-start.1 = (bf16[256,512]{1,0:T(8,128)(2,1)S(1)}, bf16[256,512]{1,0:T(8,128)(2,1)}, u32[]{:S(2)}) copy-start(bf16[256,512]{1,0:T(8,128)(2,1)} %constant.15.clone.both_low) | copy-start | bytes 786436
  3.5 0.9 %copy-start.2 = (bf16[256,512]{1,0:T(8,128)(2,1)S(1)}, bf16[256,512]{1,0:T(8,128)(2,1)}, u32[]{:S(2)}) copy-start(bf16[256,512]{1,0:T(8,128)(2,1)} %constant.14.clone.both_high) | copy-start | bytes 786436
  4.5 0.9 %copy-start.3 = (f32[3,72,192]{2,1,0:T(8,128)S(1)}, f32[3,72,192]{2,1,0:T(8,128)}, u32[]{:S(2)}) copy-start(f32[3,72,192]{2,1,0:T(8,128)} %constant.16.clone.node_tab) | copy-start | bytes 497668
  5.4 0.9 %copy-start.4 = (bf16[64,1024]{1,0:T(8,128)(2,1)S(1)}, bf16[64,1024]{1,0:T(8,128)(2,1)}, u32[]{:S(2)}) copy-start(bf16[64,1024]{1,0:T(8,128)(2,1)} %constant.18.clone.spread) | copy-start | bytes 393220

commit v2 on v1

--- a/solution.py
+++ b/solution.py
@@ -60,9 +60,10 @@
     deriv = differentiation()
     ident = np.eye(6)
     two = np.eye(2)
-    along_x = np.zeros((PAIR, 192))
-    along_y = np.zeros((PAIR, 192))
-    lift = np.zeros((PAIR, 192))
+    along_x = np.zeros((PAIR, 168))
+    along_y = np.zeros((PAIR, 168))
+    lift = np.zeros((PAIR, 168))
+    lift_x = np.zeros((PAIR, 24))
     along_x[:, 0:72] = -np.kron(two, np.kron(deriv, ident))
     along_y[:, 72:144] = -np.kron(two, np.kron(ident, deriv))
     for e in range(2):
@@ -70,7 +71,7 @@
             for j in range(6):
                 lane = e * 12 + s2 * 6 + j
                 lift[e * 36 + 6 * j + 5 * s2, 144 + lane] = 1.0
-                lift[e * 36 + 30 * s2 + j, 168 + lane] = 1.0
+                lift_x[e * 36 + 30 * s2 + j, lane] = 1.0
     tables = np.stack([along_x, along_y, lift]).astype(np.float32)
     marks = np.zeros((PAIR, 8), np.float32)
     p = np.arange(PAIR) % 36
@@ -78,7 +79,7 @@
     marks[:, 1] = 1.0 * (p % 6 == 5) - 1.0 * (p % 6 == 0)
     marks[:, 2] = np.abs(marks[:, 0])
     marks[:, 3] = np.abs(marks[:, 1])
-    return tables, marks
+    return tables, np.kron(np.eye(4), lift_x).astype(jnp.bfloat16), marks
 
 
 def lookup_tables(elems, rows):
@@ -91,6 +92,7 @@
     spread[e[used], lane[used]] = 1.0
     marks[0] = np.where(used, r % 6, 0)
     marks[1] = np.where(used, r // 6 % 2, 0)
+    marks[3] = used
     rim_spread = np.zeros((rows, LANES))
     rim_lane = np.arange(6 * rows)
     rim_spread[rim_lane // 6, rim_lane] = 1.0
@@ -138,15 +140,19 @@
             self.tiles[dt] = value
 
 
-def kernel(
-    groups, span,
-    state, metric, neighbour, orient, wall, rim,
-    both_high, both_low, node_tab, node_marks, spread, rim_spread, lane_marks,
-    out,
-    index, flip, others, rim_send, rim_recv, send_a, send_b, recv_a, recv_b,
-    fields, rows_r, back_send, back_recv,
-    rim_sems, a_sems, b_sems, back_sems,
-):
+def kernel(groups, span, *refs):
+    given, refs = refs[:14], refs[14:]
+    out, refs = refs[0], refs[1:]
+    held, refs = refs[:14], refs[14:]
+    (
+        index, flip, others, rim_send, rim_recv, send_a, send_b, recv_a, recv_b,
+        fields, rows_r, back_sum, back_send, back_recv,
+        load_sems, rim_sems, a_sems, b_sems, back_sems, hello,
+    ) = refs
+    (
+        state, neighbour, orient, wall, rim, spread, rim_spread, lane_marks,
+        metric, node_tab, node_marks, lift_x, both_high, both_low,
+    ) = held
     me = lax.axis_index("span")
     group = lax.axis_index("elem")
     lower = lax.rem(group + groups - 1, groups)
@@ -154,7 +160,10 @@
     elems = metric.shape[1]
     modes = span * 8
     state_tiles = elems * NODES // LANES
-    halves = span // 16
+
+    loads = [pltpu.make_async_copy(a, b, load_sems.at[i]) for i, (a, b) in enumerate(zip(given, held))]
+    for load in loads[:8]:
+        load.start()
 
     barrier = pltpu.get_barrier_semaphore()
 
@@ -164,48 +173,48 @@
         )
         return carry
 
+    lax.fori_loop(1, span, greet, 0)
     pl.semaphore_signal(barrier, 1, device_id=(lower, me), device_id_type=MESH)
-    pl.semaphore_signal(barrier, 1, device_id=(upper, me), device_id_type=MESH)
-    lax.fori_loop(1, span, greet, 0)
-
-    def bases(slot, reverse):
+    for load in loads[8:]:
+        load.start()
+    for load in loads[1:8]:
+        load.wait()
+
+    def bases(slot):
         side = slot & 3
         vertical = side >= 2
         step = jnp.where(vertical, 6, 1)
         first = jnp.where(vertical, jnp.where(side == 3, 5, 0), jnp.where(side == 1, 30, 0))
-        base = NODES * (slot >> 2) + first
-        return base, step
-
-    def spread_over(values, matrix, dims):
+        return NODES * (slot >> 2) + first, step
+
+    def spread_over(values, matrix):
         high = (values >> 6).astype(F32).astype(BF16)
         low = (values & 63).astype(F32).astype(BF16)
-        go = lambda x: lax.dot_general(x, matrix, (dims, ((), ())), preferred_element_type=F32)
+        go = lambda x: jnp.dot(x, matrix, preferred_element_type=F32)
         return (go(high) * 64.0 + go(low)).astype(jnp.int32)
 
-    rim_base, rim_step = bases(rim[...], None)
-    natural = ((1,), (0,))
+    rim_base, rim_step = bases(rim[...])
     node_r = lane_marks[2:3, 0:LANES].astype(jnp.int32)
-    rim_index = spread_over(rim_base, rim_spread[...], natural) + node_r * spread_over(
-        rim_step, rim_spread[...], natural
+    rim_index = spread_over(rim_base, rim_spread[...]) + node_r * spread_over(
+        rim_step, rim_spread[...]
     )
 
     slot = neighbour[...]
     turn = orient[...]
     remote = slot >= 4 * elems
-    base, step = bases(slot, None)
+    base, step = bases(slot)
     row = slot - 4 * elems
     base = jnp.where(remote, state_tiles * LANES + LANES * (row >> 4) + 6 * (row & 15), base)
     step = jnp.where(remote, 1, step)
     base = jnp.where(turn == 1, base + 5 * step, base)
     step = jnp.where(turn == 1, -step, step)
-    over = ((0,), (0,))
     matrix = spread[...]
-    base_l = spread_over(base, matrix, over)
-    step_l = spread_over(step + 64, matrix, over) - 64
-    wall_l = spread_over(wall[...], matrix, over)
+    base_l = spread_over(base, matrix)
+    step_l = spread_over(step + 8, matrix) - 8
+    wall_l = spread_over(wall[...], matrix)
     node_l = lane_marks[0:1, :].astype(jnp.int32)
     second = lane_marks[1:2, :] > 0.5
-    used = spread_over(jnp.ones_like(slot), matrix, over)[0:1] > 0
+    used = lane_marks[3:4, :] > 0.5
     for axis in range(2):
         pick = lambda x: jnp.where(second, x[2 * axis + 1 : 2 * axis + 2], x[2 * axis : 2 * axis + 1])
         lanes_at = jnp.where(used, pick(base_l) + pick(step_l) * node_l, 0)
@@ -231,6 +240,7 @@
                 totals[v] = jnp.where(here, got, totals[v])
         return totals
 
+    loads[0].wait()
     zero = [jnp.zeros((8, LANES), F32)] * 4
     for way in range(2):
         at = jnp.broadcast_to(rim_index[way : way + 1], (8, LANES))
@@ -238,19 +248,15 @@
         for v in range(4):
             rim_send[way, v] = got[v]
 
-    pl.semaphore_wait(barrier, span + 1)
-
-    rim_copies = [
-        pltpu.make_async_remote_copy(
+    def rim_copy(way, to):
+        return pltpu.make_async_remote_copy(
             rim_send.at[way], rim_recv.at[1 - way], rim_sems.at[way], rim_sems.at[3 - way],
             device_id=(to, me), device_id_type=MESH,
         )
-        for way, to in ((0, lower), (1, upper))
-    ]
-    for copy in rim_copies:
-        copy.start()
-
+
+    rim_up, rim_down = rim_copy(1, upper), rim_copy(0, lower)
     lane = lax.broadcasted_iota(jnp.int32, (8, LANES), 1)
+    row8 = lax.broadcasted_iota(jnp.int32, (8, LANES), 0)
 
     def gather_axis(axis, tiles, first):
         def one(t, carry):
@@ -294,19 +300,18 @@
         pltpu.make_async_copy(src(me), dst(me), sems.at[1]).start()
 
     mode_rows = lambda who: pl.ds(pl.multiple_of(8 * who, 8), 8)
+
+    pl.semaphore_wait(barrier, span)
+    pl.semaphore_signal(hello, 1, device_id=(upper, me), device_id_type=MESH)
+    rim_up.start()
     exchange(lambda to: send_a.at[to], lambda who: recv_a.at[mode_rows(who), :], a_sems)
 
     gather_axis(0, range(state_tiles), True)
-    for copy in rim_copies:
-        copy.wait()
-    gather_axis(0, range(state_tiles, state_tiles + 2), False)
-    for d in range(span):
-        b = Builder(lane)
-        for v in range(4):
-            b.add(("other", v), lambda k, v=v: reflected(0, v, k), 32 * d, 24 * v, 24)
-        send_b[d] = b.tiles[0]
-    exchange(lambda to: send_b.at[to], lambda who: recv_b.at[mode_rows(who), :], b_sems)
-
+    pl.semaphore_wait(hello, 1)
+    rim_down.start()
+
+    for load in loads[8:]:
+        load.wait()
     at = lax.broadcasted_iota(jnp.int32, (2, elems), 1)
     scale = metric[...]
     first = jnp.sum(jnp.where(at == 2 * me, scale, 0.0), axis=1, keepdims=True)
@@ -327,7 +332,17 @@
     toward = jnp.where(low_side, 7.5, -7.5)
     ox, oy = per_row(24, 0), per_row(24, 1)
 
-    over0 = ((0,), (0,))
+    rim_up.wait()
+    rim_down.wait()
+    gather_axis(0, range(state_tiles, state_tiles + 2), False)
+    for d in range(span):
+        b = Builder(lane)
+        for v in range(4):
+            b.add(("other", v), lambda k, v=v: reflected(0, v, k), 32 * d, 24 * v, 24)
+        send_b[d] = b.tiles[0]
+    exchange(lambda to: send_b.at[to], lambda who: recv_b.at[mode_rows(who), :], b_sems)
+
+    over0, over1 = ((0,), (0,)), ((1,), (1,))
     pltpu.make_async_copy(recv_a, recv_a, a_sems.at[1]).wait()
     basis = (both_high[:, 0:modes], both_low[:, 0:modes])
     planes_a = dot3(split(recv_a[...]), basis, over0)
@@ -340,32 +355,55 @@
         fields[v, 72:144] = own[1] * own[v]
         fields[v, 144:168] = facing_y_coef * facing_y[v]
         rows_r[72 * v : 72 * v + 72, modes : 2 * modes] = own[2] * own[v]
-        rows_r[72 * v : 72 * v + 72, 0:modes] = own_coef * own[v]
+        rows_r[72 * v : 72 * v + 72, 0:modes] = own_coef * own[v] + dot3(
+            operator, split(fields[v]), ((1,), (0,))
+        )
+    back_sum[:, 0:288] = dot3((both_high[...], both_low[...]), split(rows_r[...]), over1)
 
     pltpu.make_async_copy(recv_b, recv_b, b_sems.at[1]).wait()
-    planes_b = dot3(split(recv_b[...]), basis, over0)
-    facing_x = [planes_b[24 * v : 24 * v + 24] for v in range(4)]
-    facing_x_coef = (toward * ox) * facing_x[0] + 7.5 * jnp.abs(ox)
-    for v in range(4):
-        fields[v, 168:192] = facing_x_coef * facing_x[v]
-        rows_r[72 * v : 72 * v + 72, 0:modes] += dot3(operator, split(fields[v]), ((1,), (0,)))
-
-    back_send[:, 0:288] = dot3(
-        (both_high[...], both_low[...]), split(rows_r[...]), ((1,), (1,))
+    planes_b = dot3(split(recv_b[:, 0:96]), basis, over0)
+    facing_x_coef = (toward * ox) * planes_b[0:24] + 7.5 * jnp.abs(ox)
+    jump_high, jump_low = split(jnp.concatenate([facing_x_coef] * 4, axis=0) * planes_b)
+    lifted = [
+        jnp.dot(lift_x[...], part, preferred_element_type=F32).astype(BF16)
+        for part in (jump_high, jump_low)
+    ]
+    back_sum[:, 0:288] += dot3(basis, lifted, over1)
+
+    for d in range(span):
+        mine = back_sum[8 * d : 8 * d + 8, :]
+        back_send[18 * d : 18 * d + 8, :] = mine[:, 0:LANES]
+        back_send[18 * d + 8 : 18 * d + 16, :] = mine[:, LANES : 2 * LANES]
+        rest = jnp.take_along_axis(mine[:, 2 * LANES :], lane & 31, axis=1, mode="promise_in_bounds")
+        rest = jnp.where((lane >> 5) == (row8 & 3), rest, 0.0)
+        for a in range(2):
+            back_send[18 * d + 16 + a : 18 * d + 17 + a, :] = jnp.sum(
+                rest[4 * a : 4 * a + 4], axis=0, keepdims=True
+            )
+    message = lambda who: pl.ds(18 * who, 18)
+    exchange(
+        lambda to: back_send.at[message(to), :], lambda who: back_recv.at[message(who), :], back_sems
     )
-    exchange(lambda to: back_send.at[mode_rows(to), :], lambda who: back_recv.at[who], back_sems)
     pltpu.make_async_copy(back_recv, back_recv, back_sems.at[1]).wait()
 
-    mode = 8 * me + lax.broadcasted_iota(jnp.int32, (8, LANES), 0)
+    mode = 8 * me + row8
     k = jnp.where(mode == 1, modes // 2, mode >> 1).astype(F32)
     shrink = 1.0 / (1.0 + TIME_STEP * VISCOSITY * k * k)
+    top = row8 < 4
+    unfold = (lane & 31) + 32 * (row8 & 3)
+
+    def unfolded(s, t):
+        if t < 2:
+            return back_recv[18 * s + 8 * t : 18 * s + 8 * t + 8, :]
+        rest = jnp.where(
+            top, back_recv[18 * s + 16 : 18 * s + 17, :], back_recv[18 * s + 17 : 18 * s + 18, :]
+        )
+        return jnp.take_along_axis(rest, unfold, axis=1, mode="promise_in_bounds")
+
     builders = [Builder(lane) for _ in range(4)]
-    for d in range(span):
+    for s in range(span):
         for v in range(4):
-            builders[v].add(
-                d, lambda t, d=d: back_recv[d, :, t * LANES : (t + 1) * LANES],
-                PAIR * v, PAIR * d, PAIR,
-            )
+            builders[v].add(s, lambda t, s=s: unfolded(s, t), PAIR * v, PAIR * s, PAIR)
     for v in range(4):
         for t in range(state_tiles):
             cut = slice(t * LANES, (t + 1) * LANES)
@@ -373,21 +411,23 @@
 
     pltpu.make_async_copy(send_a.at[0 : span - 1], send_a.at[0 : span - 1], a_sems.at[0]).wait()
     pltpu.make_async_copy(send_b.at[0 : span - 1], send_b.at[0 : span - 1], b_sems.at[0]).wait()
-    sent = back_send.at[0 : 8 * (span - 1), :]
+    sent = back_send.at[0 : 18 * (span - 1), :]
     pltpu.make_async_copy(sent, sent, back_sems.at[0]).wait()
 
 
 def body(groups, span, state, metric, neighbour, orient, wall, rim):
     elems = metric.shape[1]
     modes = span * 8
-    tables, marks = node_tables()
+    tables, lift_x, marks = node_tables()
     spread, rim_spread, lane_marks = lookup_tables(elems, rim.shape[1])
     both_high, both_low = basis_tables(modes)
-    constants = [both_high, both_low, tables, marks, spread, rim_spread, lane_marks]
-    constants = [jnp.asarray(c) for c in constants]
-    vmem = pl.BlockSpec(memory_space=pltpu.VMEM)
+    given = [
+        state, neighbour.T, orient.T, wall.T, rim, spread, rim_spread, lane_marks,
+        metric, tables, marks, lift_x, both_high, both_low,
+    ]
+    given = [jnp.asarray(x) for x in given]
     gathered = elems // 2 * 32 // LANES
-    scratch = [
+    scratch = [pltpu.VMEM(x.shape, x.dtype) for x in given] + [
         pltpu.VMEM((2, gathered, 8, LANES), jnp.int32),
         pltpu.VMEM((2, gathered, 8, LANES), F32),
         pltpu.VMEM((2, 4, gathered, 8, LANES), F32),
@@ -397,26 +437,29 @@
         pltpu.VMEM((span, 8, LANES), F32),
         pltpu.VMEM((modes, 384), F32),
         pltpu.VMEM((modes, LANES), F32),
-        pltpu.VMEM((4, 192, modes), F32),
+        pltpu.VMEM((4, 168, modes), F32),
         pltpu.VMEM((288, 2 * modes), F32),
         pltpu.VMEM((modes, 384), F32),
-        pltpu.VMEM((span, 8, 384), F32),
+        pltpu.VMEM((18 * span, LANES), F32),
+        pltpu.VMEM((18 * span, LANES), F32),
+        pltpu.SemaphoreType.DMA((len(given),)),
         pltpu.SemaphoreType.DMA((4,)),
         pltpu.SemaphoreType.DMA((2,)),
         pltpu.SemaphoreType.DMA((2,)),
         pltpu.SemaphoreType.DMA((2,)),
+        pltpu.SemaphoreType.REGULAR,
     ]
     return pl.pallas_call(
         functools.partial(kernel, groups, span),
         out_shape=jax.ShapeDtypeStruct(state.shape, F32),
-        in_specs=[vmem] * 13,
-        out_specs=vmem,
+        in_specs=[pl.BlockSpec(memory_space=pltpu.HBM)] * len(given),
+        out_specs=pl.BlockSpec(memory_space=pltpu.VMEM),
         scratch_shapes=scratch,
         compiler_params=pltpu.CompilerParams(
-            collective_id=0, has_side_effects=True, vmem_limit_bytes=40 << 20
+            collective_id=0, has_side_effects=True, vmem_limit_bytes=60 << 20
         ),
         name="section",
-    )(state, metric, neighbour, orient, wall, rim, *constants)
+    )(*given)
 
 
 def solution(mesh):

time: 50.2 us -> 41.3 us (0.82)
  local copies, waits for them, and re-layouts: 6.99 us -> 1.69 us
  Pallas kernels: 42.8 us -> 39.5 us
    unnamed x28 -> x1, local copies, waits for them, and re-layouts: 6.99 us -> 1.69 us
    pallas_call x1, Pallas kernels: 42.8 us -> 39.5 us  [body(): pl.pallas_call(functools.partial(kernel, groups, span), out_shape=jax.Sha...]
where the time goes in v2:
time: 41.3 us; the launch traced here: 41.2 us
  Pallas kernels  39.5 us (96%)
  local copies, waits for them, and re-layouts  1.69 us (4%)
    pallas_call x1, Pallas kernels, body(): pl.pallas_call(functools.partial(kernel, groups, span), out_shape=jax.Sha...  39.5 us
    unnamed x1, local copies, waits for them, and re-layouts  1.69 us

profile of v2, /device:TPU:15, one launch (start us, length us, event | category | flops | bytes accessed | tf_op | source)
XLA Modules:
  0.0 41.2 jit_solution(915299577321931529)
XLA Ops:
  0.0 39.5 %section.1 = f32[4,8,2304]{2,1,0:T(8,128)} custom-call(f32[4,8,2304]{2,1,0:T(8,128)} %refs_0_.1, s32[4,64]{1,0:T(4,128)} %bitcast.3, s32[4,64]{1,0:T(4,128)} %bitcast.4, s32[4,64]{1,0:T(4,128)} %bitcast.5, s32[2,16]{1,0:T(2,128)} %refs_4_.1, bf16[64,1024]{1,0:T(8,128)(2,1)} %constant.16.clone.refs_5_, bf16[16,128]{1,0:T(8,128)(2,1)} %constant.17.clone.refs_6_, ...), custom_call_target="tpu_custom_call" | custom-call | tf_op jit(solution)/shard_map/section/pallas_call | solution.py:452
  39.5 1.7 %copy.16 = f32[4,8,2304]{2,1,0:T(8,128)} copy(f32[4,8,2304]{2,1,0:T(8,128)} %section.1) | data formatting | bytes 589824

commit v3 on v2

v3 whole, which is shorter than its diff:
```python
import functools
import math

import jax
import jax.numpy as jnp
import numpy as np
from jax import lax
from jax.experimental import pallas as pl
from jax.experimental.pallas import tpu as pltpu
from jax.sharding import PartitionSpec as P

TIME_STEP = 0.001
VISCOSITY = 0.02
MESH = pl.DeviceIdType.MESH
F32 = jnp.float32
BF16 = jnp.bfloat16
NODES = 36
PAIR = 72
LANES = 128


def differentiation():
    near = math.sqrt(1.0 / 3.0 - 2.0 * math.sqrt(7.0) / 21.0)
    far = math.sqrt(1.0 / 3.0 + 2.0 * math.sqrt(7.0) / 21.0)
    points = np.array([-1.0, -far, -near, near, far, 1.0])
    weights = np.array(
        [1.0 / np.prod([points[c] - points[s] for s in range(6) if s != c]) for c in range(6)]
    )
    deriv = np.zeros((6, 6))
    for t in range(6):
        for s in range(6):
            if s != t:
                deriv[t, s] = weights[s] / weights[t] / (points[t] - points[s])
        deriv[t, t] = -np.sum(deriv[t])
    return deriv


def split_np(x):
    high = x.astype(jnp.bfloat16)
    low = (x - high.astype(np.float64)).astype(jnp.bfloat16)
    return high, low


def basis_tables(count):
    m = np.arange(count)[:, None]
    n = np.arange(count)[None, :]
    angle = (m // 2 * n % count) * (2.0 * math.pi / count)
    basis = np.where(m % 2 == 1, np.sin(angle), np.cos(angle)) * math.sqrt(2.0 / count)
    basis[0] = 1.0 / math.sqrt(count)
    basis[1] = (1.0 - 2.0 * (np.arange(count) % 2)) / math.sqrt(count)
    minus = np.zeros_like(basis)
    k = np.arange(count // 2)[:, None]
    minus[0::2] = -k * basis[1::2]
    minus[1::2] = k * basis[0::2]
    both = np.concatenate([basis, minus], axis=1)
    return split_np(both)


def node_tables():
    deriv = differentiation()
    ident = np.eye(6)
    two = np.eye(2)
    along_x = np.zeros((PAIR, 144))
    along_y = np.zeros((PAIR, 144))
    lift = np.zeros((PAIR, 48))
    along_x[:, 0:72] = -np.kron(two, np.kron(deriv, ident))
    along_y[:, 72:144] = -np.kron(two, np.kron(ident, deriv))
    for e in range(2):
        for s2 in range(2):
            for j in range(6):
                lane = e * 12 + s2 * 6 + j
                lift[e * 36 + 6 * j + 5 * s2, lane] = 1.0
                lift[e * 36 + 30 * s2 + j, 24 + lane] = 1.0
    tables = np.stack([along_x, along_y]).astype(np.float32)
    marks = np.zeros((PAIR, 8), np.float32)
    p = np.arange(PAIR) % 36
    marks[:, 0] = 1.0 * (p // 6 == 5) - 1.0 * (p // 6 == 0)
    marks[:, 1] = 1.0 * (p % 6 == 5) - 1.0 * (p % 6 == 0)
    marks[:, 2] = np.abs(marks[:, 0])
    marks[:, 3] = np.abs(marks[:, 1])
    return tables, np.kron(np.eye(4), lift).astype(jnp.bfloat16), marks


def lookup_tables(elems, rows):
    spread = np.zeros((elems, elems // 2 * 32))
    marks = np.zeros((8, elems // 2 * 32), np.float32)
    lane = np.arange(elems // 2 * 32)
    r = lane % 32
    used = r < 24
    e = 2 * (lane // 32) + r % 24 // 12
    spread[e[used], lane[used]] = 1.0
    marks[0] = np.where(used, r % 6, 0)
    marks[1] = np.where(used, r // 6 % 2, 0)
    marks[3] = used
    rim_spread = np.zeros((rows, LANES))
    rim_lane = np.arange(6 * rows)
    rim_spread[rim_lane // 6, rim_lane] = 1.0
    marks[2, : 6 * rows] = rim_lane % 6
    return spread.astype(jnp.bfloat16), rim_spread.astype(jnp.bfloat16), marks


def split(x):
    high = x.astype(BF16)
    low = (x - high.astype(F32)).astype(BF16)
    return high, low


def dot3(a, b, dims):
    go = lambda x, y: lax.dot_general(x, y, (dims, ((), ())), preferred_element_type=F32)
    return go(a[0], b[0]) + (go(a[0], b[1]) + go(a[1], b[0]))


def pieces(src, dst, length):
    out = []
    done = 0
    while done < length:
        s, d = src + done, dst + done
        size = min(length - done, LANES - s % LANES, LANES - d % LANES)
        out.append((s // LANES, d // LANES, (d - s) % LANES, d % LANES, d % LANES + size))
        done += size
    return out


class Builder:
    def __init__(self, lane):
        self.lane = lane
        self.tiles = {}
        self.turned = {}

    def add(self, key, load, src, dst, length):
        for st, dt, shift, lo, hi in pieces(src, dst, length):
            name = (key, st, shift)
            if name not in self.turned:
                tile = load(st)
                self.turned[name] = pltpu.roll(tile, shift, 1) if shift else tile
            value = self.turned[name]
            if dt in self.tiles:
                value = jnp.where((self.lane >= lo) & (self.lane < hi), value, self.tiles[dt])
            self.tiles[dt] = value


OWN_ROWS = 18
FACING_ROWS = 12


def kernel(groups, span, *refs):
    given, refs = refs[:14], refs[14:]
    out, refs = refs[0], refs[1:]
    held, refs = refs[:14], refs[14:]
    (
        index, flip, others, rim_send, rim_recv, send_a, send_b, recv_a, recv_b, coef_a, coef_b,
        fields, rows_r, back_sum, back_send, back_recv,
        load_sems, rim_sems, a_sems, b_sems, back_sems, hello,
    ) = refs
    (
        state, rim, rim_spread, lane_marks, neighbour, orient, wall, spread,
        metric, node_tab, node_marks, lift, both_high, both_low,
    ) = held
    me = lax.axis_index("span")
    group = lax.axis_index("elem")
    lower = lax.rem(group + groups - 1, groups)
    upper = lax.rem(group + 1, groups)
    elems = metric.shape[1]
    modes = span * 8
    state_tiles = elems * NODES // LANES

    loads = [pltpu.make_async_copy(a, b, load_sems.at[i]) for i, (a, b) in enumerate(zip(given, held))]
    for load in loads[:4]:
        load.start()

    barrier = pltpu.get_barrier_semaphore()

    def greet(k, carry):
        pl.semaphore_signal(
            barrier, 1, device_id=(group, lax.rem(me + k, span)), device_id_type=MESH
        )
        return carry

    pl.semaphore_signal(barrier, 1, device_id=(lower, me), device_id_type=MESH)
    lax.fori_loop(1, span, greet, 0)
    for load in loads[4:]:
        load.start()

    lane = lax.broadcasted_iota(jnp.int32, (8, LANES), 1)
    row8 = lax.broadcasted_iota(jnp.int32, (8, LANES), 0)

    def bases(slot):
        side = slot & 3
        vertical = side >= 2
        step = jnp.where(vertical, 6, 1)
        first = jnp.where(vertical, jnp.where(side == 3, 5, 0), jnp.where(side == 1, 30, 0))
        return NODES * (slot >> 2) + first, step

    def spread_over(values, matrix):
        high = (values >> 6).astype(F32).astype(BF16)
        low = (values & 63).astype(F32).astype(BF16)
        go = lambda x: jnp.dot(x, matrix, preferred_element_type=F32)
        return (go(high) * 64.0 + go(low)).astype(jnp.int32)

    def picked(tile, at):
        return jnp.take_along_axis(tile, at, axis=1, mode="promise_in_bounds")

    def gather(at, start, tiles):
        low = at & (LANES - 1)
        high = at >> 7
        totals = list(start)
        for k in tiles:
            here = high == k
            for v in range(4):
                tile = (
                    state[v, :, k * LANES : (k + 1) * LANES]
                    if k < state_tiles
                    else rim_recv[k - state_tiles, v]
                )
                totals[v] = jnp.where(here, picked(tile, low), totals[v])
        return totals

    def fold(tile, width, store):
        every = LANES // width
        tile = jnp.where(lane // width == (row8 & (every - 1)), picked(tile, lane & (width - 1)), 0.0)
        for a in range(8 // every):
            store(a, jnp.sum(tile[every * a : every * (a + 1)], axis=0, keepdims=True))

    def unfold(load, width):
        every = LANES // width
        tile = load(0)
        for a in range(1, 8 // every):
            tile = jnp.where(row8 < every * a, tile, load(a))
        return picked(jnp.broadcast_to(tile, (8, LANES)), (lane & (width - 1)) + width * (row8 & (every - 1)))

    for load in loads[1:4]:
        load.wait()
    rim_base, rim_step = bases(rim[...])
    node_r = lane_marks[2:3, 0:LANES].astype(jnp.int32)
    rim_index = spread_over(rim_base, rim_spread[...]) + node_r * spread_over(
        rim_step, rim_spread[...]
    )
    loads[0].wait()
    zero = [jnp.zeros((8, LANES), F32)] * 4
    for way in range(2):
        at = jnp.broadcast_to(rim_index[way : way + 1], (8, LANES))
        got = gather(at, zero, range(state_tiles))
        for v in range(4):
            rim_send[way, v] = got[v]

    def rim_copy(way, to):
        return pltpu.make_async_remote_copy(
            rim_send.at[way], rim_recv.at[1 - way], rim_sems.at[way], rim_sems.at[3 - way],
            device_id=(to, me), device_id_type=MESH,
        )

    rim_up, rim_down = rim_copy(1, upper), rim_copy(0, lower)
    pl.semaphore_wait(barrier, span)
    pl.semaphore_signal(hello, 1, device_id=(upper, me), device_id_type=MESH)
    rim_up.start()

    def exchange(send, recv, rows, sems, near=None):
        arrived = sems.at[1] if near is None else sems.at[1 + near]
        at = lambda who: pl.ds(rows * who, rows)

        def one(k, carry):
            to = lax.rem(me + k, span)
            pltpu.make_async_remote_copy(
                send.at[at(to), :], recv.at[at(me), :], sems.at[0], arrived,
                device_id=(group, to), device_id_type=MESH,
            ).start()
            return carry

        lax.fori_loop(1, span, one, 0)
        pltpu.make_async_copy(send.at[at(me), :], recv.at[at(me), :], arrived).start()

    for d in range(span):
        b = Builder(lane)
        for v in range(4):
            b.add(v, lambda k, v=v: state[v, :, k * LANES : (k + 1) * LANES], PAIR * d, PAIR * v, PAIR)
        top = OWN_ROWS * d
        send_a[top : top + 8, :] = b.tiles[0]
        send_a[top + 8 : top + 16, :] = b.tiles[1]

        def store(a, row, top=top):
            send_a[top + 16 + a : top + 17 + a, :] = row

        fold(b.tiles[2], 32, store)

    @pl.when(group > 0)
    def _():
        pl.semaphore_wait(hello, 1)
        rim_down.start()

    exchange(send_a, recv_a, OWN_ROWS, a_sems)

    for load in loads[4:8]:
        load.wait()
    slot = neighbour[...]
    turn = orient[...]
    remote = slot >= 4 * elems
    base, step = bases(slot)
    row = slot - 4 * elems
    base = jnp.where(remote, state_tiles * LANES + LANES * (row >> 4) + 6 * (row & 15), base)
    step = jnp.where(remote, 1, step)
    base = jnp.where(turn == 1, base + 5 * step, base)
    step = jnp.where(turn == 1, -step, step)
    matrix = spread[...]
    base_l = spread_over(base, matrix)
    step_l = spread_over(step + 8, matrix) - 8
    wall_l = spread_over(wall[...], matrix)
    node_l = lane_marks[0:1, :].astype(jnp.int32)
    second = lane_marks[1:2, :] > 0.5
    used = lane_marks[3:4, :] > 0.5
    for axis in range(2):
        pick = lambda x: jnp.where(second, x[2 * axis + 1 : 2 * axis + 2], x[2 * axis : 2 * axis + 1])
        lanes_at = jnp.where(used, pick(base_l) + pick(step_l) * node_l, 0)
        walls = 1.0 - 2.0 * pick(wall_l).astype(F32)
        for t in range(index.shape[1]):
            cut = slice(t * LANES, (t + 1) * LANES)
            index[axis, t] = jnp.broadcast_to(lanes_at[:, cut], (8, LANES))
            flip[axis, t] = jnp.broadcast_to(walls[:, cut], (8, LANES))

    def gather_axis(axis, tiles, first):
        def one(t, carry):
            at = index[axis, t]
            start = zero if first else [others[axis, v, t] for v in range(4)]
            got = gather(at, start, tiles)
            for v in range(4):
                others[axis, v, t] = got[v]
            return carry

        lax.fori_loop(0, index.shape[1], one, 0)

    gather_axis(0, range(state_tiles), True)
    gather_axis(1, range(state_tiles), True)

    @pl.when(group == 0)
    def _():
        pl.semaphore_wait(hello, 1)
        rim_down.start()

    rim_up.wait()
    rim_down.wait()
    gather_axis(0, range(state_tiles, state_tiles + 2), False)

    def reflected(axis, v, t):
        tile = others[axis, v, t]
        return tile * flip[axis, t] if v < 3 else tile

    for d in range(span):
        b = Builder(lane)
        for v in range(4):
            for axis in range(2):
                b.add(
                    (axis, v), lambda k, a=axis, v=v: reflected(a, v, k),
                    32 * d, 48 * v + 24 * (1 - axis), 24,
                )
        top = FACING_ROWS * d
        send_b[top : top + 8, :] = b.tiles[0]

        def store(a, row, top=top):
            send_b[top + 8 + a : top + 9 + a, :] = row

        fold(b.tiles[1], 64, store)
    exchange(send_b, recv_b, FACING_ROWS, b_sems)

    for load in loads[8:]:
        load.wait()
    at = lax.broadcasted_iota(jnp.int32, (2, elems), 1)
    scale = metric[...]
    first = jnp.sum(jnp.where(at == 2 * me, scale, 0.0), axis=1, keepdims=True)
    last = jnp.sum(jnp.where(at == 2 * me + 1, scale, 0.0), axis=1, keepdims=True)

    def per_row(rows, which):
        e = lax.broadcasted_iota(jnp.int32, (rows, 1), 0)
        return jnp.where(e < rows // 2, first[which : which + 1], last[which : which + 1])

    rx, ry = per_row(PAIR, 0), per_row(PAIR, 1)
    marks = node_marks[...]
    coef_u = 7.5 * rx * marks[:, 0:1]
    coef_v = 7.5 * ry * marks[:, 1:2]
    coef_c = 7.5 * (jnp.abs(rx) * marks[:, 2:3] + jnp.abs(ry) * marks[:, 3:4])
    operator = split(rx * node_tab[0] + ry * node_tab[1])
    side = lax.broadcasted_iota(jnp.int32, (24, 1), 0)
    low_side = (side < 6) | ((side >= 12) & (side < 18))
    toward = jnp.where(low_side, 7.5, -7.5)
    ox, oy = per_row(24, 0), per_row(24, 1)

    over0, over1 = ((0,), (0,)), ((1,), (1,))
    basis = (both_high[:, 0:modes], both_low[:, 0:modes])
    pltpu.make_async_copy(recv_a, recv_a, a_sems.at[1]).wait()
    for s in range(span):
        top = OWN_ROWS * s
        cut = slice(8 * s, 8 * s + 8)
        coef_a[cut, 0:LANES] = recv_a[top : top + 8, :]
        coef_a[cut, LANES : 2 * LANES] = recv_a[top + 8 : top + 16, :]
        coef_a[cut, 2 * LANES :] = unfold(lambda a: recv_a[top + 16 + a : top + 17 + a, :], 32)
    planes_a = dot3(split(coef_a[:, 0:288]), basis, over0)
    own = [planes_a[PAIR * v : PAIR * (v + 1)] for v in range(4)]
    own_coef = coef_u * own[0] + coef_v * own[1] - coef_c
    for v in range(4):
        fields[v, 0:72] = own[0] * own[v]
        fields[v, 72:144] = own[1] * own[v]
        rows_r[72 * v : 72 * v + 72, modes : 2 * modes] = own[2] * own[v]
        rows_r[72 * v : 72 * v + 72, 0:modes] = own_coef * own[v] + dot3(
            operator, split(fields[v]), ((1,), (0,))
        )
    back_sum[:, 0:288] = dot3((both_high[...], both_low[...]), split(rows_r[...]), over1)

    pltpu.make_async_copy(recv_b, recv_b, b_sems.at[1]).wait()
    for s in range(span):
        top = FACING_ROWS * s
        cut = slice(8 * s, 8 * s + 8)
        coef_b[cut, 0:LANES] = recv_b[top : top + 8, :]
        coef_b[cut, LANES:] = unfold(lambda a: recv_b[top + 8 + a : top + 9 + a, :], 64)
    planes_b = dot3(split(coef_b[:, 0:192]), basis, over0)
    facing_coef = jnp.concatenate(
        [
            (toward * oy) * planes_b[48:72] + 7.5 * jnp.abs(oy),
            (toward * ox) * planes_b[24:48] + 7.5 * jnp.abs(ox),
        ],
        axis=0,
    )
    jump_high, jump_low = split(jnp.concatenate([facing_coef] * 4, axis=0) * planes_b)
    lifted = split(
        jnp.dot(lift[...], jump_high, preferred_element_type=F32)
        + jnp.dot(lift[...], jump_low, preferred_element_type=F32)
    )
    back_sum[:, 0:288] += dot3(basis, lifted, over1)

    for d in range(span):
        top = OWN_ROWS * d
        mine = back_sum[8 * d : 8 * d + 8, :]
        back_send[top : top + 8, :] = mine[:, 0:LANES]
        back_send[top + 8 : top + 16, :] = mine[:, LANES : 2 * LANES]

        def store(a, row, top=top):
            back_send[top + 16 + a : top + 17 + a, :] = row

        fold(mine[:, 2 * LANES :], 32, store)
    half = span // 2
    near = me // half
    exchange(back_send, back_recv, OWN_ROWS, back_sems, near)

    mode = 8 * me + row8
    k = jnp.where(mode == 1, modes // 2, mode >> 1).astype(F32)
    shrink = 1.0 / (1.0 + TIME_STEP * VISCOSITY * k * k)

    def finish(i, carry):
        h = lax.rem(near + i, 2)
        part = back_recv.at[pl.ds(pl.multiple_of(OWN_ROWS * half * h, 8), OWN_ROWS * half), :]
        pltpu.make_async_copy(part, part, back_sems.at[1 + h]).wait()
        builders = [Builder(lane) for _ in range(4)]

        def back(s, t):
            top = OWN_ROWS * s
            if t < 2:
                return part[top + 8 * t : top + 8 * t + 8, :]
            return unfold(lambda a: part[top + 16 + a : top + 17 + a, :], 32)

        for s in range(half):
            for v in range(4):
                builders[v].add(s, lambda t, s=s: back(s, t), PAIR * v, PAIR * s, PAIR)
        for v in range(4):
            for t in range(state_tiles // 2):
                cut = pl.ds(pl.multiple_of((state_tiles // 2 * h + t) * LANES, LANES), LANES)
                out[v, :, cut] = (state[v, :, cut] + TIME_STEP * builders[v].tiles[t]) * shrink
        return carry

    lax.fori_loop(0, 2, finish, 0)

    for send, rows, sems in (
        (send_a, OWN_ROWS, a_sems), (send_b, FACING_ROWS, b_sems), (back_send, OWN_ROWS, back_sems),
    ):
        sent = send.at[0 : rows * (span - 1), :]
        pltpu.make_async_copy(sent, sent, sems.at[0]).wait()


def body(groups, span, state, metric, neighbour, orient, wall, rim):
    elems = metric.shape[1]
    modes = span * 8
    tables, lift, marks = node_tables()
    spread, rim_spread, lane_marks = lookup_tables(elems, rim.shape[1])
    both_high, both_low = basis_tables(modes)
    given = [
        state, rim, rim_spread, lane_marks, neighbour.T, orient.T, wall.T, spread,
        metric, tables, marks, lift, both_high, both_low,
    ]
    given = [jnp.asarray(x) for x in given]
    gathered = elems // 2 * 32 // LANES
    scratch = [pltpu.VMEM(x.shape, x.dtype) for x in given] + [
        pltpu.VMEM((2, gathered, 8, LANES), jnp.int32),
        pltpu.VMEM((2, gathered, 8, LANES), F32),
        pltpu.VMEM((2, 4, gathered, 8, LANES), F32),
        pltpu.VMEM((2, 4, 8, LANES), F32),
        pltpu.VMEM((2, 4, 8, LANES), F32),
        pltpu.VMEM((OWN_ROWS * span, LANES), F32),
        pltpu.VMEM((FACING_ROWS * span, LANES), F32),
        pltpu.VMEM((OWN_ROWS * span, LANES), F32),
        pltpu.VMEM((FACING_ROWS * span, LANES), F32),
        pltpu.VMEM((modes, 384), F32),
        pltpu.VMEM((modes, 256), F32),
        pltpu.VMEM((4, 144, modes), F32),
        pltpu.VMEM((288, 2 * modes), F32),
        pltpu.VMEM((modes, 384), F32),
        pltpu.VMEM((OWN_ROWS * span, LANES), F32),
        pltpu.VMEM((OWN_ROWS * span, LANES), F32),
        pltpu.SemaphoreType.DMA((len(given),)),
        pltpu.SemaphoreType.DMA((4,)),
        pltpu.SemaphoreType.DMA((2,)),
        pltpu.SemaphoreType.DMA((2,)),
        pltpu.SemaphoreType.DMA((3,)),
        pltpu.SemaphoreType.REGULAR,
    ]
    return pl.pallas_call(
        functools.partial(kernel, groups, span),
        out_shape=jax.ShapeDtypeStruct(state.shape, F32),
        in_specs=[pl.BlockSpec(memory_space=pltpu.HBM)] * len(given),
        out_specs=pl.BlockSpec(memory_space=pltpu.VMEM),
        scratch_shapes=scratch,
        compiler_params=pltpu.CompilerParams(
            collective_id=0, has_side_effects=True, vmem_limit_bytes=60 << 20
        ),
        name="section",
    )(*given)


def solution(mesh):
    specs = (
        P(None, "span", "elem"), P(None, "elem"), P("elem", None),
        P("elem", None), P("elem", None), P(None, "elem"),
    )
    return jax.shard_map(
        functools.partial(body, mesh.shape["elem"], mesh.shape["span"]),
        mesh=mesh, in_specs=specs, out_specs=P(None, "span", "elem"), check_vma=False,
    )
```

time: 41.3 us -> 41.6 us (level)
  the two profiles are of different devices: /device:TPU:15 before, /device:TPU:1 now
where the time goes in v3:
time: 41.6 us; the launch traced here: 41.3 us
  Pallas kernels  39.6 us (95%)
  local copies, waits for them, and re-layouts  1.69 us (4%)
    pallas_call x1, Pallas kernels, body(): pl.pallas_call(functools.partial(kernel, groups, span), out_shape=jax.Sha...  39.6 us
    unnamed x1, local copies, waits for them, and re-layouts  1.69 us

profile of v3, /device:TPU:1, one launch (start us, length us, event | category | flops | bytes accessed | tf_op | source)
XLA Modules:
  0.0 41.3 jit_solution(1942365199117072462)
XLA Ops:
  0.0 39.6 %section.1 = f32[4,8,2304]{2,1,0:T(8,128)} custom-call(f32[4,8,2304]{2,1,0:T(8,128)} %refs_0_.1, s32[2,16]{1,0:T(2,128)} %refs_1_.1, bf16[16,128]{1,0:T(8,128)(2,1)} %constant.16.clone.refs_2_, f32[8,1024]{1,0:T(8,128)} %constant.17.clone.refs_3_, s32[4,64]{1,0:T(4,128)} %bitcast.3, s32[4,64]{1,0:T(4,128)} %bitcast.4, s32[4,64]{1,0:T(4,128)} %bitcast.5, ...), custom_call_target="tpu_custom_call" | custom-call | tf_op jit(solution)/shard_map/section/pallas_call | solution.py:511
  39.6 1.7 %copy.16 = f32[4,8,2304]{2,1,0:T(8,128)} copy(f32[4,8,2304]{2,1,0:T(8,128)} %section.1) | data formatting | bytes 589824

commit v4 on v3

--- a/solution.py
+++ b/solution.py
@@ -17,6 +17,8 @@
 NODES = 36
 PAIR = 72
 LANES = 128
+INNER = ((6, 30), (42, 66))
+OUTER = ((0, 6), (30, 36), (36, 42), (66, 72))
 
 
 def differentiation():
@@ -60,25 +62,26 @@
     deriv = differentiation()
     ident = np.eye(6)
     two = np.eye(2)
-    along_x = np.zeros((PAIR, 144))
-    along_y = np.zeros((PAIR, 144))
-    lift = np.zeros((PAIR, 48))
-    along_x[:, 0:72] = -np.kron(two, np.kron(deriv, ident))
-    along_y[:, 72:144] = -np.kron(two, np.kron(ident, deriv))
+    along_x = np.zeros((PAIR, 168))
+    along_y = np.zeros((PAIR, 168))
+    lift = np.zeros((PAIR, 168))
+    order = np.concatenate([np.arange(a, b) for a, b in INNER + OUTER])
+    along_x[:, 0:72] = -np.kron(two, np.kron(deriv, ident))[order][:, order]
+    along_y[:, 72:144] = -np.kron(two, np.kron(ident, deriv))[order][:, order]
     for e in range(2):
         for s2 in range(2):
             for j in range(6):
-                lane = e * 12 + s2 * 6 + j
-                lift[e * 36 + 6 * j + 5 * s2, lane] = 1.0
-                lift[e * 36 + 30 * s2 + j, 24 + lane] = 1.0
-    tables = np.stack([along_x, along_y]).astype(np.float32)
+                lift[e * 36 + 6 * j + 5 * s2, 144 + e * 12 + s2 * 6 + j] = 1.0
+    lift = lift[order]
+    tables = np.stack([along_x, along_y, lift]).astype(np.float32)
     marks = np.zeros((PAIR, 8), np.float32)
-    p = np.arange(PAIR) % 36
+    p = order % 36
     marks[:, 0] = 1.0 * (p // 6 == 5) - 1.0 * (p // 6 == 0)
     marks[:, 1] = 1.0 * (p % 6 == 5) - 1.0 * (p % 6 == 0)
     marks[:, 2] = np.abs(marks[:, 0])
     marks[:, 3] = np.abs(marks[:, 1])
-    return tables, np.kron(np.eye(4), lift).astype(jnp.bfloat16), marks
+    marks[:, 4] = order >= 36
+    return tables, marks
 
 
 def lookup_tables(elems, rows):
@@ -139,22 +142,22 @@
             self.tiles[dt] = value
 
 
-OWN_ROWS = 18
-FACING_ROWS = 12
+INNER_ROWS = 12
+OUTER_ROWS = 6
 
 
 def kernel(groups, span, *refs):
-    given, refs = refs[:14], refs[14:]
+    given, refs = refs[:13], refs[13:]
     out, refs = refs[0], refs[1:]
-    held, refs = refs[:14], refs[14:]
+    held, refs = refs[:13], refs[13:]
     (
-        index, flip, others, rim_send, rim_recv, send_a, send_b, recv_a, recv_b, coef_a, coef_b,
-        fields, rows_r, back_sum, back_send, back_recv,
-        load_sems, rim_sems, a_sems, b_sems, back_sems, hello,
+        index, flip, others, rim_send, rim_recv, send_a, send_b, send_c, recv_a, recv_b, recv_c,
+        modal_c, fields, rows_r, inner_sum, outer_sum, inner_send, outer_send, inner_recv, outer_recv, change,
+        load_sems, rim_sems, a_sems, b_sems, c_sems, inner_sems, outer_sems, hello,
     ) = refs
     (
         state, rim, rim_spread, lane_marks, neighbour, orient, wall, spread,
-        metric, node_tab, node_marks, lift, both_high, both_low,
+        metric, node_tab, node_marks, both_high, both_low,
     ) = held
     me = lax.axis_index("span")
     group = lax.axis_index("elem")
@@ -215,9 +218,10 @@
                 totals[v] = jnp.where(here, picked(tile, low), totals[v])
         return totals
 
-    def fold(tile, width, store):
+    def fold(tile, start, width, store):
         every = LANES // width
-        tile = jnp.where(lane // width == (row8 & (every - 1)), picked(tile, lane & (width - 1)), 0.0)
+        tile = picked(tile, start + (lane & (width - 1)))
+        tile = jnp.where(lane // width == (row8 & (every - 1)), tile, 0.0)
         for a in range(8 // every):
             store(a, jnp.sum(tile[every * a : every * (a + 1)], axis=0, keepdims=True))
 
@@ -227,6 +231,19 @@
         for a in range(1, 8 // every):
             tile = jnp.where(row8 < every * a, tile, load(a))
         return picked(jnp.broadcast_to(tile, (8, LANES)), (lane & (width - 1)) + width * (row8 & (every - 1)))
+
+    def fold_96(tile, store):
+        fold(tile, 0, 64, store)
+        fold(tile, 64, 32, lambda a, row: store(4 + a, row))
+
+    def unfold_96(load):
+        return jnp.where(lane < 64, unfold(load, 64), unfold(lambda a: load(4 + a), 32))
+
+    def rows_of(ref, top):
+        def store(a, row):
+            ref[top + a : top + a + 1, :] = row
+
+        return store, lambda a: ref[top + a : top + a + 1, :]
 
     for load in loads[1:4]:
         load.wait()
@@ -250,13 +267,22 @@
         )
 
     rim_up, rim_down = rim_copy(1, upper), rim_copy(0, lower)
+    for d in range(span):
+        b = Builder(lane)
+        for v in range(4):
+            b.add(v, lambda k, v=v: state[v, :, k * LANES : (k + 1) * LANES], PAIR * d, PAIR * v, PAIR)
+        rows = slice(8 * d, 8 * d + 8)
+        send_a[rows, 0:LANES] = b.tiles[0]
+        send_a[rows, LANES:] = b.tiles[1]
+        send_b[rows, :] = b.tiles[2]
+
     pl.semaphore_wait(barrier, span)
     pl.semaphore_signal(hello, 1, device_id=(upper, me), device_id_type=MESH)
     rim_up.start()
 
-    def exchange(send, recv, rows, sems, near=None):
-        arrived = sems.at[1] if near is None else sems.at[1 + near]
-        at = lambda who: pl.ds(rows * who, rows)
+    def exchange(send, recv, rows, sems):
+        arrived = sems.at[1]
+        at = lambda who: pl.ds(pl.multiple_of(rows * who, 8) if rows == 8 else rows * who, rows)
 
         def one(k, carry):
             to = lax.rem(me + k, span)
@@ -269,25 +295,12 @@
         lax.fori_loop(1, span, one, 0)
         pltpu.make_async_copy(send.at[at(me), :], recv.at[at(me), :], arrived).start()
 
-    for d in range(span):
-        b = Builder(lane)
-        for v in range(4):
-            b.add(v, lambda k, v=v: state[v, :, k * LANES : (k + 1) * LANES], PAIR * d, PAIR * v, PAIR)
-        top = OWN_ROWS * d
-        send_a[top : top + 8, :] = b.tiles[0]
-        send_a[top + 8 : top + 16, :] = b.tiles[1]
-
-        def store(a, row, top=top):
-            send_a[top + 16 + a : top + 17 + a, :] = row
-
-        fold(b.tiles[2], 32, store)
-
     @pl.when(group > 0)
     def _():
         pl.semaphore_wait(hello, 1)
         rim_down.start()
 
-    exchange(send_a, recv_a, OWN_ROWS, a_sems)
+    exchange(send_a, recv_a, 8, a_sems)
 
     for load in loads[4:8]:
         load.wait()
@@ -327,8 +340,19 @@
 
         lax.fori_loop(0, index.shape[1], one, 0)
 
+    def reflected(axis, v, t):
+        tile = others[axis, v, t]
+        return tile * flip[axis, t] if v < 3 else tile
+
+    gather_axis(1, range(state_tiles), True)
+    for d in range(span):
+        b = Builder(lane)
+        b.tiles[0] = send_b[8 * d : 8 * d + 8, :]
+        for v in range(4):
+            b.add(v, lambda k, v=v: reflected(1, v, k), 32 * d, 32 + 24 * v, 24)
+        send_b[8 * d : 8 * d + 8, :] = b.tiles[0]
+    exchange(send_b, recv_b, 8, b_sems)
     gather_axis(0, range(state_tiles), True)
-    gather_axis(1, range(state_tiles), True)
 
     @pl.when(group == 0)
     def _():
@@ -339,26 +363,12 @@
     rim_down.wait()
     gather_axis(0, range(state_tiles, state_tiles + 2), False)
 
-    def reflected(axis, v, t):
-        tile = others[axis, v, t]
-        return tile * flip[axis, t] if v < 3 else tile
-
     for d in range(span):
         b = Builder(lane)
         for v in range(4):
-            for axis in range(2):
-                b.add(
-                    (axis, v), lambda k, a=axis, v=v: reflected(a, v, k),
-                    32 * d, 48 * v + 24 * (1 - axis), 24,
-                )
-        top = FACING_ROWS * d
-        send_b[top : top + 8, :] = b.tiles[0]
-
-        def store(a, row, top=top):
-            send_b[top + 8 + a : top + 9 + a, :] = row
-
-        fold(b.tiles[1], 64, store)
-    exchange(send_b, recv_b, FACING_ROWS, b_sems)
+            b.add(v, lambda k, v=v: reflected(0, v, k), 32 * d, 24 * v, 24)
+        fold_96(b.tiles[0], rows_of(send_c, OUTER_ROWS * d)[0])
+    exchange(send_c, recv_c, OUTER_ROWS, c_sems)
 
     for load in loads[8:]:
         load.wait()
@@ -367,106 +377,105 @@
     first = jnp.sum(jnp.where(at == 2 * me, scale, 0.0), axis=1, keepdims=True)
     last = jnp.sum(jnp.where(at == 2 * me + 1, scale, 0.0), axis=1, keepdims=True)
 
-    def per_row(rows, which):
-        e = lax.broadcasted_iota(jnp.int32, (rows, 1), 0)
-        return jnp.where(e < rows // 2, first[which : which + 1], last[which : which + 1])
-
-    rx, ry = per_row(PAIR, 0), per_row(PAIR, 1)
+    def per_row(on_first, which):
+        return jnp.where(on_first, first[which : which + 1], last[which : which + 1])
+
     marks = node_marks[...]
+    on_first = marks[:, 4:5] < 0.5
+    rx, ry = per_row(on_first, 0), per_row(on_first, 1)
     coef_u = 7.5 * rx * marks[:, 0:1]
     coef_v = 7.5 * ry * marks[:, 1:2]
     coef_c = 7.5 * (jnp.abs(rx) * marks[:, 2:3] + jnp.abs(ry) * marks[:, 3:4])
-    operator = split(rx * node_tab[0] + ry * node_tab[1])
+    operator = split(rx * node_tab[0] + ry * node_tab[1] + node_tab[2])
     side = lax.broadcasted_iota(jnp.int32, (24, 1), 0)
     low_side = (side < 6) | ((side >= 12) & (side < 18))
     toward = jnp.where(low_side, 7.5, -7.5)
-    ox, oy = per_row(24, 0), per_row(24, 1)
+    ox, oy = per_row(side < 12, 0), per_row(side < 12, 1)
 
     over0, over1 = ((0,), (0,)), ((1,), (1,))
     basis = (both_high[:, 0:modes], both_low[:, 0:modes])
     pltpu.make_async_copy(recv_a, recv_a, a_sems.at[1]).wait()
-    for s in range(span):
-        top = OWN_ROWS * s
-        cut = slice(8 * s, 8 * s + 8)
-        coef_a[cut, 0:LANES] = recv_a[top : top + 8, :]
-        coef_a[cut, LANES : 2 * LANES] = recv_a[top + 8 : top + 16, :]
-        coef_a[cut, 2 * LANES :] = unfold(lambda a: recv_a[top + 16 + a : top + 17 + a, :], 32)
-    planes_a = dot3(split(coef_a[:, 0:288]), basis, over0)
-    own = [planes_a[PAIR * v : PAIR * (v + 1)] for v in range(4)]
+    planes_a = dot3(split(recv_a[...]), basis, over0)
+    pltpu.make_async_copy(recv_b, recv_b, b_sems.at[1]).wait()
+    planes_b = dot3(split(recv_b[...]), basis, over0)
+    own = [planes_a[PAIR * v : PAIR * (v + 1)] for v in range(3)]
+    own.append(jnp.concatenate([planes_a[3 * PAIR :], planes_b[0:32]], axis=0))
+    own = [jnp.concatenate([x[a:b] for a, b in INNER + OUTER], axis=0) for x in own]
+    facing_y = [planes_b[32 + 24 * v : 56 + 24 * v] for v in range(4)]
     own_coef = coef_u * own[0] + coef_v * own[1] - coef_c
+    facing_y_coef = (toward * oy) * facing_y[1] + 7.5 * jnp.abs(oy)
     for v in range(4):
         fields[v, 0:72] = own[0] * own[v]
         fields[v, 72:144] = own[1] * own[v]
-        rows_r[72 * v : 72 * v + 72, modes : 2 * modes] = own[2] * own[v]
-        rows_r[72 * v : 72 * v + 72, 0:modes] = own_coef * own[v] + dot3(
-            operator, split(fields[v]), ((1,), (0,))
-        )
-    back_sum[:, 0:288] = dot3((both_high[...], both_low[...]), split(rows_r[...]), over1)
-
-    pltpu.make_async_copy(recv_b, recv_b, b_sems.at[1]).wait()
+        fields[v, 144:168] = facing_y_coef * facing_y[v]
+        along_z = own[2] * own[v]
+        planar = own_coef * own[v] + dot3(operator, split(fields[v]), ((1,), (0,)))
+        for part, at in ((planar, slice(0, modes)), (along_z, slice(modes, 2 * modes))):
+            rows_r[48 * v : 48 * v + 48, at] = part[0:48]
+            rows_r[192 + 24 * v : 216 + 24 * v, at] = part[48:72]
+    both = (both_high[...], both_low[...])
+
+    inner_sum[:, 0:192] = dot3(both, split(rows_r[0:192, :]), over1)
+    for d in range(span):
+        mine = inner_sum[8 * d : 8 * d + 8, :]
+        top = INNER_ROWS * d
+        inner_send[top : top + 8, :] = mine[:, 0:LANES]
+        fold(mine[:, LANES:], 0, 64, rows_of(inner_send, top + 8)[0])
+    exchange(inner_send, inner_recv, INNER_ROWS, inner_sems)
+    outer_sum[:, 0:96] = dot3(both, split(rows_r[192:288, :]), over1)
+
+    pltpu.make_async_copy(recv_c, recv_c, c_sems.at[1]).wait()
     for s in range(span):
-        top = FACING_ROWS * s
-        cut = slice(8 * s, 8 * s + 8)
-        coef_b[cut, 0:LANES] = recv_b[top : top + 8, :]
-        coef_b[cut, LANES:] = unfold(lambda a: recv_b[top + 8 + a : top + 9 + a, :], 64)
-    planes_b = dot3(split(coef_b[:, 0:192]), basis, over0)
-    facing_coef = jnp.concatenate(
-        [
-            (toward * oy) * planes_b[48:72] + 7.5 * jnp.abs(oy),
-            (toward * ox) * planes_b[24:48] + 7.5 * jnp.abs(ox),
-        ],
-        axis=0,
-    )
-    jump_high, jump_low = split(jnp.concatenate([facing_coef] * 4, axis=0) * planes_b)
-    lifted = split(
-        jnp.dot(lift[...], jump_high, preferred_element_type=F32)
-        + jnp.dot(lift[...], jump_low, preferred_element_type=F32)
-    )
-    back_sum[:, 0:288] += dot3(basis, lifted, over1)
-
+        modal_c[8 * s : 8 * s + 8, :] = unfold_96(rows_of(recv_c, OUTER_ROWS * s)[1])
+    planes_c = dot3(split(modal_c[:, 0:96]), basis, over0)
+    facing_x_coef = (toward * ox) * planes_c[0:24] + 7.5 * jnp.abs(ox)
+    jump = split(jnp.concatenate([facing_x_coef] * 4, axis=0) * planes_c)
+    outer_sum[:, 0:96] += dot3(basis, jump, over1)
     for d in range(span):
-        top = OWN_ROWS * d
-        mine = back_sum[8 * d : 8 * d + 8, :]
-        back_send[top : top + 8, :] = mine[:, 0:LANES]
-        back_send[top + 8 : top + 16, :] = mine[:, LANES : 2 * LANES]
-
-        def store(a, row, top=top):
-            back_send[top + 16 + a : top + 17 + a, :] = row
-
-        fold(mine[:, 2 * LANES :], 32, store)
-    half = span // 2
-    near = me // half
-    exchange(back_send, back_recv, OWN_ROWS, back_sems, near)
+        fold_96(outer_sum[8 * d : 8 * d + 8, :], rows_of(outer_send, OUTER_ROWS * d)[0])
+    exchange(outer_send, outer_recv, OUTER_ROWS, outer_sems)
 
     mode = 8 * me + row8
     k = jnp.where(mode == 1, modes // 2, mode >> 1).astype(F32)
     shrink = 1.0 / (1.0 + TIME_STEP * VISCOSITY * k * k)
 
-    def finish(i, carry):
-        h = lax.rem(near + i, 2)
-        part = back_recv.at[pl.ds(pl.multiple_of(OWN_ROWS * half * h, 8), OWN_ROWS * half), :]
-        pltpu.make_async_copy(part, part, back_sems.at[1 + h]).wait()
-        builders = [Builder(lane) for _ in range(4)]
-
-        def back(s, t):
-            top = OWN_ROWS * s
-            if t < 2:
-                return part[top + 8 * t : top + 8 * t + 8, :]
-            return unfold(lambda a: part[top + 16 + a : top + 17 + a, :], 32)
-
-        for s in range(half):
-            for v in range(4):
-                builders[v].add(s, lambda t, s=s: back(s, t), PAIR * v, PAIR * s, PAIR)
+    pltpu.make_async_copy(inner_recv, inner_recv, inner_sems.at[1]).wait()
+    builders = [Builder(lane) for _ in range(4)]
+    for s in range(span):
+        top = INNER_ROWS * s
+
+        def inner(t, top=top):
+            if t == 0:
+                return inner_recv[top : top + 8, :]
+            return unfold(rows_of(inner_recv, top + 8)[1], 64)
+
+        tiles = [inner(0), inner(1)]
         for v in range(4):
-            for t in range(state_tiles // 2):
-                cut = pl.ds(pl.multiple_of((state_tiles // 2 * h + t) * LANES, LANES), LANES)
-                out[v, :, cut] = (state[v, :, cut] + TIME_STEP * builders[v].tiles[t]) * shrink
-        return carry
-
-    lax.fori_loop(0, 2, finish, 0)
+            for e, (a, b) in enumerate(INNER):
+                builders[v].add((s, e), lambda t, x=tiles: x[t], 48 * v + 24 * e, PAIR * s + a, 24)
+    for v in range(4):
+        for t in range(state_tiles):
+            cut = slice(t * LANES, (t + 1) * LANES)
+            change[v, :, cut] = builders[v].tiles[t]
+
+    pltpu.make_async_copy(outer_recv, outer_recv, outer_sems.at[1]).wait()
+    builders = [Builder(lane) for _ in range(4)]
+    for v in range(4):
+        for t in range(state_tiles):
+            builders[v].tiles[t] = change[v, :, t * LANES : (t + 1) * LANES]
+    for s in range(span):
+        tile = unfold_96(rows_of(outer_recv, OUTER_ROWS * s)[1])
+        for v in range(4):
+            for src, dst, length in ((0, 0, 6), (6, 30, 12), (18, 66, 6)):
+                builders[v].add((s, src), lambda t, x=tile: x, 24 * v + src, PAIR * s + dst, length)
+    for v in range(4):
+        for t in range(state_tiles):
+            cut = slice(t * LANES, (t + 1) * LANES)
+            out[v, :, cut] = (state[v, :, cut] + TIME_STEP * builders[v].tiles[t]) * shrink
 
     for send, rows, sems in (
-        (send_a, OWN_ROWS, a_sems), (send_b, FACING_ROWS, b_sems), (back_send, OWN_ROWS, back_sems),
+        (send_a, 8, a_sems), (send_b, 8, b_sems), (send_c, OUTER_ROWS, c_sems),
+        (inner_send, INNER_ROWS, inner_sems), (outer_send, OUTER_ROWS, outer_sems),
     ):
         sent = send.at[0 : rows * (span - 1), :]
         pltpu.make_async_copy(sent, sent, sems.at[0]).wait()
@@ -475,12 +484,12 @@
 def body(groups, span, state, metric, neighbour, orient, wall, rim):
     elems = metric.shape[1]
     modes = span * 8
-    tables, lift, marks = node_tables()
+    tables, marks = node_tables()
     spread, rim_spread, lane_marks = lookup_tables(elems, rim.shape[1])
     both_high, both_low = basis_tables(modes)
     given = [
         state, rim, rim_spread, lane_marks, neighbour.T, orient.T, wall.T, spread,
-        metric, tables, marks, lift, both_high, both_low,
+        metric, tables, marks, both_high, both_low,
     ]
     given = [jnp.asarray(x) for x in given]
     gathered = elems // 2 * 32 // LANES
@@ -490,22 +499,29 @@
         pltpu.VMEM((2, 4, gathered, 8, LANES), F32),
         pltpu.VMEM((2, 4, 8, LANES), F32),
         pltpu.VMEM((2, 4, 8, LANES), F32),
-        pltpu.VMEM((OWN_ROWS * span, LANES), F32),
-        pltpu.VMEM((FACING_ROWS * span, LANES), F32),
-        pltpu.VMEM((OWN_ROWS * span, LANES), F32),
-        pltpu.VMEM((FACING_ROWS * span, LANES), F32),
-        pltpu.VMEM((modes, 384), F32),
         pltpu.VMEM((modes, 256), F32),
-        pltpu.VMEM((4, 144, modes), F32),
+        pltpu.VMEM((modes, LANES), F32),
+        pltpu.VMEM((OUTER_ROWS * span, LANES), F32),
+        pltpu.VMEM((modes, 256), F32),
+        pltpu.VMEM((modes, LANES), F32),
+        pltpu.VMEM((OUTER_ROWS * span, LANES), F32),
+        pltpu.VMEM((modes, LANES), F32),
+        pltpu.VMEM((4, 168, modes), F32),
         pltpu.VMEM((288, 2 * modes), F32),
-        pltpu.VMEM((modes, 384), F32),
-        pltpu.VMEM((OWN_ROWS * span, LANES), F32),
-        pltpu.VMEM((OWN_ROWS * span, LANES), F32),
+        pltpu.VMEM((modes, 256), F32),
+        pltpu.VMEM((modes, LANES), F32),
+        pltpu.VMEM((INNER_ROWS * span, LANES), F32),
+        pltpu.VMEM((OUTER_ROWS * span, LANES), F32),
+        pltpu.VMEM((INNER_ROWS * span, LANES), F32),
+        pltpu.VMEM((OUTER_ROWS * span, LANES), F32),
+        pltpu.VMEM(state.shape, F32),
         pltpu.SemaphoreType.DMA((len(given),)),
         pltpu.SemaphoreType.DMA((4,)),
         pltpu.SemaphoreType.DMA((2,)),
         pltpu.SemaphoreType.DMA((2,)),
-        pltpu.SemaphoreType.DMA((3,)),
+        pltpu.SemaphoreType.DMA((2,)),
+        pltpu.SemaphoreType.DMA((2,)),
+        pltpu.SemaphoreType.DMA((2,)),
         pltpu.SemaphoreType.REGULAR,
     ]
     return pl.pallas_call(

time: 41.6 us -> 39.2 us (0.942)
  Pallas kernels: 39.6 us -> 37.4 us
    pallas_call x1, Pallas kernels: 39.6 us -> 37.4 us  [body(): pl.pallas_call(functools.partial(kernel, groups, span), out_shape=jax.Sha...]
where the time goes in v4:
time: 39.2 us; the launch traced here: 39.1 us
  Pallas kernels  37.4 us (95%)
  local copies, waits for them, and re-layouts  1.69 us (4%)
    pallas_call x1, Pallas kernels, body(): pl.pallas_call(functools.partial(kernel, groups, span), out_shape=jax.Sha...  37.4 us
    unnamed x1, local copies, waits for them, and re-layouts  1.69 us

profile of v4, /device:TPU:1, one launch (start us, length us, event | category | flops | bytes accessed | tf_op | source)
XLA Modules:
  0.0 39.1 jit_solution(2918088799132359875)
XLA Ops:
  0.0 37.4 %section.1 = f32[4,8,2304]{2,1,0:T(8,128)} custom-call(f32[4,8,2304]{2,1,0:T(8,128)} %refs_0_.1, s32[2,16]{1,0:T(2,128)} %refs_1_.1, bf16[16,128]{1,0:T(8,128)(2,1)} %constant.14.clone.refs_2_, f32[8,1024]{1,0:T(8,128)} %constant.15.clone.refs_3_, s32[4,64]{1,0:T(4,128)} %bitcast.3, s32[4,64]{1,0:T(4,128)} %bitcast.4, s32[4,64]{1,0:T(4,128)} %bitcast.5, ...), custom_call_target="tpu_custom_call" | custom-call | tf_op jit(solution)/shard_map/section/pallas_call | solution.py:527
  37.4 1.7 %copy.15 = f32[4,8,2304]{2,1,0:T(8,128)} copy(f32[4,8,2304]{2,1,0:T(8,128)} %section.1) | data formatting | bytes 589824

commit v5 on v4

--- a/solution.py
+++ b/solution.py
@@ -142,18 +142,61 @@
             self.tiles[dt] = value
 
 
+def picked(tile, at):
+    return jnp.take_along_axis(tile, at, axis=1, mode="promise_in_bounds")
+
+
+def tile_indices():
+    return tuple(lax.broadcasted_iota(jnp.int32, (8, LANES), dim) for dim in range(2))
+
+
+def fold(tile, start, width, store):
+    row8, lane = tile_indices()
+    every = LANES // width
+    tile = picked(tile, start + (lane & (width - 1)))
+    tile = jnp.where(lane // width == (row8 & (every - 1)), tile, 0.0)
+    for a in range(8 // every):
+        store(a, jnp.sum(tile[every * a : every * (a + 1)], axis=0, keepdims=True))
+
+
+def unfold(load, width):
+    row8, lane = tile_indices()
+    every = LANES // width
+    tile = load(0)
+    for a in range(1, 8 // every):
+        tile = jnp.where(row8 < every * a, tile, load(a))
+    return picked(jnp.broadcast_to(tile, (8, LANES)), (lane & (width - 1)) + width * (row8 & (every - 1)))
+
+
+def fold_96(tile, store):
+    fold(tile, 0, 64, store)
+    fold(tile, 64, 32, lambda a, row: store(4 + a, row))
+
+
+def unfold_96(load):
+    lane = tile_indices()[1]
+    return jnp.where(lane < 64, unfold(load, 64), unfold(lambda a: load(4 + a), 32))
+
+
+def rows_of(ref, top):
+    def store(a, row):
+        ref[top + a : top + a + 1, :] = row
+
+    return store, lambda a: ref[top + a : top + a + 1, :]
+
+
 INNER_ROWS = 12
 OUTER_ROWS = 6
 
 
 def kernel(groups, span, *refs):
     given, refs = refs[:13], refs[13:]
-    out, refs = refs[0], refs[1:]
+    (result, outer_recv), refs = refs[:2], refs[2:]
     held, refs = refs[:13], refs[13:]
     (
         index, flip, others, rim_send, rim_recv, send_a, send_b, send_c, recv_a, recv_b, recv_c,
-        modal_c, fields, rows_r, inner_sum, outer_sum, inner_send, outer_send, inner_recv, outer_recv, change,
-        load_sems, rim_sems, a_sems, b_sems, c_sems, inner_sems, outer_sems, hello,
+        modal_c, fields, rows_r, inner_sum, outer_sum, inner_send, outer_send, inner_recv, settled,
+        load_sems, rim_sems, a_sems, b_sems, c_sems, inner_sems, outer_sems, result_sem, hello,
     ) = refs
     (
         state, rim, rim_spread, lane_marks, neighbour, orient, wall, spread,
@@ -199,9 +242,6 @@
         low = (values & 63).astype(F32).astype(BF16)
         go = lambda x: jnp.dot(x, matrix, preferred_element_type=F32)
         return (go(high) * 64.0 + go(low)).astype(jnp.int32)
-
-    def picked(tile, at):
-        return jnp.take_along_axis(tile, at, axis=1, mode="promise_in_bounds")
 
     def gather(at, start, tiles):
         low = at & (LANES - 1)
@@ -217,33 +257,6 @@
                 )
                 totals[v] = jnp.where(here, picked(tile, low), totals[v])
         return totals
-
-    def fold(tile, start, width, store):
-        every = LANES // width
-        tile = picked(tile, start + (lane & (width - 1)))
-        tile = jnp.where(lane // width == (row8 & (every - 1)), tile, 0.0)
-        for a in range(8 // every):
-            store(a, jnp.sum(tile[every * a : every * (a + 1)], axis=0, keepdims=True))
-
-    def unfold(load, width):
-        every = LANES // width
-        tile = load(0)
-        for a in range(1, 8 // every):
-            tile = jnp.where(row8 < every * a, tile, load(a))
-        return picked(jnp.broadcast_to(tile, (8, LANES)), (lane & (width - 1)) + width * (row8 & (every - 1)))
-
-    def fold_96(tile, store):
-        fold(tile, 0, 64, store)
-        fold(tile, 64, 32, lambda a, row: store(4 + a, row))
-
-    def unfold_96(load):
-        return jnp.where(lane < 64, unfold(load, 64), unfold(lambda a: load(4 + a), 32))
-
-    def rows_of(ref, top):
-        def store(a, row):
-            ref[top + a : top + a + 1, :] = row
-
-        return store, lambda a: ref[top + a : top + a + 1, :]
 
     for load in loads[1:4]:
         load.wait()
@@ -415,7 +428,13 @@
             rows_r[192 + 24 * v : 216 + 24 * v, at] = part[48:72]
     both = (both_high[...], both_low[...])
 
-    inner_sum[:, 0:192] = dot3(both, split(rows_r[0:192, :]), over1)
+    def damped(mode):
+        k = jnp.where(mode == 1, modes // 2, mode >> 1).astype(F32)
+        return 1.0 / (1.0 + TIME_STEP * VISCOSITY * k * k)
+
+    step_of = TIME_STEP * damped(lax.broadcasted_iota(jnp.int32, (modes, 1), 0))
+
+    inner_sum[:, 0:192] = step_of * dot3(both, split(rows_r[0:192, :]), over1)
     for d in range(span):
         mine = inner_sum[8 * d : 8 * d + 8, :]
         top = INNER_ROWS * d
@@ -430,17 +449,17 @@
     planes_c = dot3(split(modal_c[:, 0:96]), basis, over0)
     facing_x_coef = (toward * ox) * planes_c[0:24] + 7.5 * jnp.abs(ox)
     jump = split(jnp.concatenate([facing_x_coef] * 4, axis=0) * planes_c)
-    outer_sum[:, 0:96] += dot3(basis, jump, over1)
+    outer_sum[:, 0:96] = step_of * (outer_sum[:, 0:96] + dot3(basis, jump, over1))
     for d in range(span):
         fold_96(outer_sum[8 * d : 8 * d + 8, :], rows_of(outer_send, OUTER_ROWS * d)[0])
     exchange(outer_send, outer_recv, OUTER_ROWS, outer_sems)
 
-    mode = 8 * me + row8
-    k = jnp.where(mode == 1, modes // 2, mode >> 1).astype(F32)
-    shrink = 1.0 / (1.0 + TIME_STEP * VISCOSITY * k * k)
-
+    shrink = damped(8 * me + row8)
     pltpu.make_async_copy(inner_recv, inner_recv, inner_sems.at[1]).wait()
+    nothing = jnp.zeros((8, LANES), F32)
     builders = [Builder(lane) for _ in range(4)]
+    for v in range(4):
+        builders[v].tiles = {t: nothing for t in range(state_tiles)}
     for s in range(span):
         top = INNER_ROWS * s
 
@@ -456,22 +475,11 @@
     for v in range(4):
         for t in range(state_tiles):
             cut = slice(t * LANES, (t + 1) * LANES)
-            change[v, :, cut] = builders[v].tiles[t]
-
+            settled[v, :, cut] = state[v, :, cut] * shrink + builders[v].tiles[t]
+    put = pltpu.make_async_copy(settled, result, result_sem)
+    put.start()
     pltpu.make_async_copy(outer_recv, outer_recv, outer_sems.at[1]).wait()
-    builders = [Builder(lane) for _ in range(4)]
-    for v in range(4):
-        for t in range(state_tiles):
-            builders[v].tiles[t] = change[v, :, t * LANES : (t + 1) * LANES]
-    for s in range(span):
-        tile = unfold_96(rows_of(outer_recv, OUTER_ROWS * s)[1])
-        for v in range(4):
-            for src, dst, length in ((0, 0, 6), (6, 30, 12), (18, 66, 6)):
-                builders[v].add((s, src), lambda t, x=tile: x, 24 * v + src, PAIR * s + dst, length)
-    for v in range(4):
-        for t in range(state_tiles):
-            cut = slice(t * LANES, (t + 1) * LANES)
-            out[v, :, cut] = (state[v, :, cut] + TIME_STEP * builders[v].tiles[t]) * shrink
+    put.wait()
 
     for send, rows, sems in (
         (send_a, 8, a_sems), (send_b, 8, b_sems), (send_c, OUTER_ROWS, c_sems),
@@ -479,6 +487,35 @@
     ):
         sent = send.at[0 : rows * (span - 1), :]
         pltpu.make_async_copy(sent, sent, sems.at[0]).wait()
+
+
+def finish(span, base, outer, out, base_v, outer_v, out_v, load_sems, store_sems):
+    loads = [
+        pltpu.make_async_copy(a, b, load_sems.at[i])
+        for i, (a, b) in enumerate(((outer, outer_v), (base, base_v)))
+    ]
+    for load in loads:
+        load.start()
+    loads[0].wait()
+    lane = tile_indices()[1]
+    tiles = [unfold_96(rows_of(outer_v, OUTER_ROWS * s)[1]) for s in range(span)]
+    loads[1].wait()
+    stores = []
+    for v in range(4):
+        b = Builder(lane)
+        for t in range(base.shape[2] // LANES):
+            b.tiles[t] = jnp.zeros((8, LANES), F32)
+        for s in range(span):
+            for src, dst, length in ((0, 0, 6), (6, 30, 12), (18, 66, 6)):
+                b.add((s, src), lambda t, x=tiles[s]: x, 24 * v + src, PAIR * s + dst, length)
+        for t in range(base.shape[2] // LANES):
+            cut = slice(t * LANES, (t + 1) * LANES)
+            out_v[v, :, cut] = base_v[v, :, cut] + b.tiles[t]
+        store = pltpu.make_async_copy(out_v.at[v], out.at[v], store_sems.at[v])
+        store.start()
+        stores.append(store)
+    for store in stores:
+        store.wait()
 
 
 def body(groups, span, state, metric, neighbour, orient, wall, rim):
@@ -513,7 +550,6 @@
         pltpu.VMEM((INNER_ROWS * span, LANES), F32),
         pltpu.VMEM((OUTER_ROWS * span, LANES), F32),
         pltpu.VMEM((INNER_ROWS * span, LANES), F32),
-        pltpu.VMEM((OUTER_ROWS * span, LANES), F32),
         pltpu.VMEM(state.shape, F32),
         pltpu.SemaphoreType.DMA((len(given),)),
         pltpu.SemaphoreType.DMA((4,)),
@@ -522,19 +558,35 @@
         pltpu.SemaphoreType.DMA((2,)),
         pltpu.SemaphoreType.DMA((2,)),
         pltpu.SemaphoreType.DMA((2,)),
+        pltpu.SemaphoreType.DMA,
         pltpu.SemaphoreType.REGULAR,
     ]
-    return pl.pallas_call(
+    hbm = pl.BlockSpec(memory_space=pltpu.HBM)
+    outer = jax.ShapeDtypeStruct((OUTER_ROWS * span, LANES), F32)
+    whole = jax.ShapeDtypeStruct(state.shape, F32)
+    base, outer_rows = pl.pallas_call(
         functools.partial(kernel, groups, span),
-        out_shape=jax.ShapeDtypeStruct(state.shape, F32),
-        in_specs=[pl.BlockSpec(memory_space=pltpu.HBM)] * len(given),
-        out_specs=pl.BlockSpec(memory_space=pltpu.VMEM),
+        out_shape=(whole, outer),
+        in_specs=[hbm] * len(given),
+        out_specs=(hbm, hbm),
         scratch_shapes=scratch,
         compiler_params=pltpu.CompilerParams(
             collective_id=0, has_side_effects=True, vmem_limit_bytes=60 << 20
         ),
         name="section",
     )(*given)
+    return pl.pallas_call(
+        functools.partial(finish, span),
+        out_shape=whole,
+        in_specs=[hbm, hbm],
+        out_specs=hbm,
+        scratch_shapes=[
+            pltpu.VMEM(whole.shape, F32), pltpu.VMEM(outer.shape, F32), pltpu.VMEM(whole.shape, F32),
+            pltpu.SemaphoreType.DMA((2,)), pltpu.SemaphoreType.DMA((4,)),
+        ],
+        compiler_params=pltpu.CompilerParams(vmem_limit_bytes=60 << 20),
+        name="finish",
+    )(base, outer_rows)
 
 
 def solution(mesh):

time: 39.2 us -> 37.9 us (0.967); the launches traced: 39.1 us -> 37.3 us
  local copies, waits for them, and re-layouts: 1.69 us -> 0 us
    unnamed x1 -> x0, local copies, waits for them, and re-layouts: 1.69 us -> none
    pallas_call x1 -> x2, Pallas kernels: 37.4 us -> 37.3 us  [the longest x1 35.3 us: body(): pl.pallas_call(functools.partial(kernel, groups, span), out_shape=(whole,...]
where the time goes in v5:
time: 37.9 us; the launch traced here: 37.3 us
  Pallas kernels  37.3 us (98%)
    pallas_call x1, Pallas kernels, body(): pl.pallas_call(functools.partial(kernel, groups, span), out_shape=(whole,...  35.3 us
    pallas_call x1, Pallas kernels, body(): pl.pallas_call(functools.partial(finish, span), out_shape=whole, in_specs...  1.99 us

profile of v5, /device:TPU:1, one launch (start us, length us, event | category | flops | bytes accessed | tf_op | source)
XLA Modules:
  0.0 37.3 jit_solution(6316210733172451783)
XLA Ops:
  0.0 35.3 %section.1 = (f32[4,8,2304]{2,1,0:T(8,128)}, f32[192,128]{1,0:T(8,128)}) custom-call(f32[4,8,2304]{2,1,0:T(8,128)} %refs_0_.1, s32[2,16]{1,0:T(2,128)} %refs_1_.1, bf16[16,128]{1,0:T(8,128)(2,1)} %constant.14.clone.refs_2_, f32[8,1024]{1,0:T(8,128)} %constant.15.clone.refs_3_, s32[4,64]{1,0:T(4,128)} %bitcast.3, s32[4,64]{1,0:T(4,128)} %bitcast.4, ...), custom_call_target="tpu_custom_call" | custom-call | tf_op jit(solution)/shard_map/section/pallas_call | solution.py:567
  35.3 2.0 %finish.1 = f32[4,8,2304]{2,1,0:T(8,128)} custom-call(f32[4,8,2304]{2,1,0:T(8,128)} %get-tuple-element.7.base, f32[192,128]{1,0:T(8,128)} %get-tuple-element.8.outer), custom_call_target="tpu_custom_call" | custom-call | tf_op jit(solution)/shard_map/finish/pallas_call | solution.py:578

commit v6 on v5

--- a/solution.py
+++ b/solution.py
@@ -308,12 +308,13 @@
         lax.fori_loop(1, span, one, 0)
         pltpu.make_async_copy(send.at[at(me), :], recv.at[at(me), :], arrived).start()
 
+    exchange(send_a, recv_a, 8, a_sems)
+
     @pl.when(group > 0)
     def _():
         pl.semaphore_wait(hello, 1)
         rim_down.start()
 
-    exchange(send_a, recv_a, 8, a_sems)
 
     for load in loads[4:8]:
         load.wait()

time: 37.9 us -> 37.1 us (0.979); the launches traced: 37.3 us -> 36.9 us
  Pallas kernels: 37.3 us -> 36.9 us
where the time goes in v6:
time: 37.1 us; the launch traced here: 36.9 us
  Pallas kernels  36.9 us (99%)
    pallas_call x1, Pallas kernels, body(): pl.pallas_call(functools.partial(kernel, groups, span), out_shape=(whole,...  34.9 us
    pallas_call x1, Pallas kernels, body(): pl.pallas_call(functools.partial(finish, span), out_shape=whole, in_specs...  1.99 us

profile of v6, /device:TPU:1, one launch (start us, length us, event | category | flops | bytes accessed | tf_op | source)
XLA Modules:
  0.0 36.9 jit_solution(14555271083783179252)
XLA Ops:
  0.0 34.9 %section.1 = (f32[4,8,2304]{2,1,0:T(8,128)}, f32[192,128]{1,0:T(8,128)}) custom-call(f32[4,8,2304]{2,1,0:T(8,128)} %refs_0_.1, s32[2,16]{1,0:T(2,128)} %refs_1_.1, bf16[16,128]{1,0:T(8,128)(2,1)} %constant.14.clone.refs_2_, f32[8,1024]{1,0:T(8,128)} %constant.15.clone.refs_3_, s32[4,64]{1,0:T(4,128)} %bitcast.3, s32[4,64]{1,0:T(4,128)} %bitcast.4, ...), custom_call_target="tpu_custom_call" | custom-call | tf_op jit(solution)/shard_map/section/pallas_call | solution.py:568
  34.9 2.0 %finish.1 = f32[4,8,2304]{2,1,0:T(8,128)} custom-call(f32[4,8,2304]{2,1,0:T(8,128)} %get-tuple-element.7.base, f32[192,128]{1,0:T(8,128)} %get-tuple-element.8.outer), custom_call_target="tpu_custom_call" | custom-call | tf_op jit(solution)/shard_map/finish/pallas_call | solution.py:579

commit v7 on v6

--- a/solution.py
+++ b/solution.py
@@ -400,7 +400,9 @@
     coef_u = 7.5 * rx * marks[:, 0:1]
     coef_v = 7.5 * ry * marks[:, 1:2]
     coef_c = 7.5 * (jnp.abs(rx) * marks[:, 2:3] + jnp.abs(ry) * marks[:, 3:4])
-    operator = split(rx * node_tab[0] + ry * node_tab[1] + node_tab[2])
+    operator = split(rx * node_tab[0, :, 0:144] + ry * node_tab[1, :, 0:144])
+    lift_y = node_tab[2, :, 144:168].astype(BF16)
+    over1_0 = ((1,), (0,))
     side = lax.broadcasted_iota(jnp.int32, (24, 1), 0)
     low_side = (side < 6) | ((side >= 12) & (side < 18))
     toward = jnp.where(low_side, 7.5, -7.5)
@@ -410,23 +412,30 @@
     basis = (both_high[:, 0:modes], both_low[:, 0:modes])
     pltpu.make_async_copy(recv_a, recv_a, a_sems.at[1]).wait()
     planes_a = dot3(split(recv_a[...]), basis, over0)
+    reorder = lambda x: jnp.concatenate([x[a:b] for a, b in INNER + OUTER], axis=0)
+    own = [reorder(planes_a[PAIR * v : PAIR * (v + 1)]) for v in range(3)]
+    own_coef = coef_u * own[0] + coef_v * own[1] - coef_c
+
+    def own_terms(v):
+        fields[v, 0:72] = own[0] * own[v]
+        fields[v, 72:144] = own[1] * own[v]
+        planar = own_coef * own[v] + dot3(operator, split(fields[v]), over1_0)
+        for part, at in ((planar, slice(0, modes)), (own[2] * own[v], slice(modes, 2 * modes))):
+            rows_r[48 * v : 48 * v + 48, at] = part[0:48]
+            rows_r[192 + 24 * v : 216 + 24 * v, at] = part[48:72]
+
+    for v in range(3):
+        own_terms(v)
     pltpu.make_async_copy(recv_b, recv_b, b_sems.at[1]).wait()
     planes_b = dot3(split(recv_b[...]), basis, over0)
-    own = [planes_a[PAIR * v : PAIR * (v + 1)] for v in range(3)]
-    own.append(jnp.concatenate([planes_a[3 * PAIR :], planes_b[0:32]], axis=0))
-    own = [jnp.concatenate([x[a:b] for a, b in INNER + OUTER], axis=0) for x in own]
-    facing_y = [planes_b[32 + 24 * v : 56 + 24 * v] for v in range(4)]
-    own_coef = coef_u * own[0] + coef_v * own[1] - coef_c
-    facing_y_coef = (toward * oy) * facing_y[1] + 7.5 * jnp.abs(oy)
+    own.append(reorder(jnp.concatenate([planes_a[3 * PAIR :], planes_b[0:32]], axis=0)))
+    facing_y_coef = (toward * oy) * planes_b[56:80] + 7.5 * jnp.abs(oy)
+    facing_y = [split(facing_y_coef * planes_b[32 + 24 * v : 56 + 24 * v]) for v in range(4)]
+    own_terms(3)
     for v in range(4):
-        fields[v, 0:72] = own[0] * own[v]
-        fields[v, 72:144] = own[1] * own[v]
-        fields[v, 144:168] = facing_y_coef * facing_y[v]
-        along_z = own[2] * own[v]
-        planar = own_coef * own[v] + dot3(operator, split(fields[v]), ((1,), (0,)))
-        for part, at in ((planar, slice(0, modes)), (along_z, slice(modes, 2 * modes))):
-            rows_r[48 * v : 48 * v + 48, at] = part[0:48]
-            rows_r[192 + 24 * v : 216 + 24 * v, at] = part[48:72]
+        lifted = sum(jnp.dot(lift_y, part, preferred_element_type=F32) for part in facing_y[v])
+        rows_r[48 * v : 48 * v + 48, 0:modes] += lifted[0:48]
+        rows_r[192 + 24 * v : 216 + 24 * v, 0:modes] += lifted[48:72]
     both = (both_high[...], both_low[...])
 
     def damped(mode):
@@ -544,7 +553,7 @@
         pltpu.VMEM((modes, LANES), F32),
         pltpu.VMEM((OUTER_ROWS * span, LANES), F32),
         pltpu.VMEM((modes, LANES), F32),
-        pltpu.VMEM((4, 168, modes), F32),
+        pltpu.VMEM((4, 144, modes), F32),
         pltpu.VMEM((288, 2 * modes), F32),
         pltpu.VMEM((modes, 256), F32),
         pltpu.VMEM((modes, LANES), F32),

time: 37.1 us -> 37.1 us (level)
  no operation moved by 1% of the time
where the time goes in v7:
time: 37.1 us; the launch traced here: 36.9 us
  Pallas kernels  36.9 us (99%)
    pallas_call x1, Pallas kernels, body(): pl.pallas_call(functools.partial(kernel, groups, span), out_shape=(whole,...  34.9 us
    pallas_call x1, Pallas kernels, body(): pl.pallas_call(functools.partial(finish, span), out_shape=whole, in_specs...  1.99 us

profile of v7, /device:TPU:1, one launch (start us, length us, event | category | flops | bytes accessed | tf_op | source)
XLA Modules:
  0.0 36.9 jit_solution(8303133049846670864)
XLA Ops:
  0.0 34.9 %section.1 = (f32[4,8,2304]{2,1,0:T(8,128)}, f32[192,128]{1,0:T(8,128)}) custom-call(f32[4,8,2304]{2,1,0:T(8,128)} %refs_0_.1, s32[2,16]{1,0:T(2,128)} %refs_1_.1, bf16[16,128]{1,0:T(8,128)(2,1)} %constant.14.clone.refs_2_, f32[8,1024]{1,0:T(8,128)} %constant.15.clone.refs_3_, s32[4,64]{1,0:T(4,128)} %bitcast.3, s32[4,64]{1,0:T(4,128)} %bitcast.4, ...), custom_call_target="tpu_custom_call" | custom-call | tf_op jit(solution)/shard_map/section/pallas_call | solution.py:577
  34.9 2.0 %finish.1 = f32[4,8,2304]{2,1,0:T(8,128)} custom-call(f32[4,8,2304]{2,1,0:T(8,128)} %get-tuple-element.7.base, f32[192,128]{1,0:T(8,128)} %get-tuple-element.8.outer), custom_call_target="tpu_custom_call" | custom-call | tf_op jit(solution)/shard_map/finish/pallas_call | solution.py:588

commit v8 on v7

--- a/solution.py
+++ b/solution.py
@@ -502,14 +502,13 @@
 def finish(span, base, outer, out, base_v, outer_v, out_v, load_sems, store_sems):
     loads = [
         pltpu.make_async_copy(a, b, load_sems.at[i])
-        for i, (a, b) in enumerate(((outer, outer_v), (base, base_v)))
+        for i, (a, b) in enumerate([(outer, outer_v)] + [(base.at[v], base_v.at[v]) for v in range(4)])
     ]
     for load in loads:
         load.start()
     loads[0].wait()
     lane = tile_indices()[1]
     tiles = [unfold_96(rows_of(outer_v, OUTER_ROWS * s)[1]) for s in range(span)]
-    loads[1].wait()
     stores = []
     for v in range(4):
         b = Builder(lane)
@@ -518,6 +517,7 @@
         for s in range(span):
             for src, dst, length in ((0, 0, 6), (6, 30, 12), (18, 66, 6)):
                 b.add((s, src), lambda t, x=tiles[s]: x, 24 * v + src, PAIR * s + dst, length)
+        loads[1 + v].wait()
         for t in range(base.shape[2] // LANES):
             cut = slice(t * LANES, (t + 1) * LANES)
             out_v[v, :, cut] = base_v[v, :, cut] + b.tiles[t]
@@ -592,7 +592,7 @@
         out_specs=hbm,
         scratch_shapes=[
             pltpu.VMEM(whole.shape, F32), pltpu.VMEM(outer.shape, F32), pltpu.VMEM(whole.shape, F32),
-            pltpu.SemaphoreType.DMA((2,)), pltpu.SemaphoreType.DMA((4,)),
+            pltpu.SemaphoreType.DMA((5,)), pltpu.SemaphoreType.DMA((4,)),
         ],
         compiler_params=pltpu.CompilerParams(vmem_limit_bytes=60 << 20),
         name="finish",

time: 37.1 us -> 37.2 us (level)
  no operation moved by 1% of the time
where the time goes in v8:
time: 37.2 us; the launch traced here: 37.1 us
  Pallas kernels  37.1 us (100%)
    pallas_call x1, Pallas kernels, body(): pl.pallas_call(functools.partial(kernel, groups, span), out_shape=(whole,...  34.9 us
    pallas_call x1, Pallas kernels, body(): pl.pallas_call(functools.partial(finish, span), out_shape=whole, in_specs...  2.15 us

profile of v8, /device:TPU:1, one launch (start us, length us, event | category | flops | bytes accessed | tf_op | source)
XLA Modules:
  0.0 37.1 jit_solution(7929768189037546651)
XLA Ops:
  0.0 34.9 %section.1 = (f32[4,8,2304]{2,1,0:T(8,128)}, f32[192,128]{1,0:T(8,128)}) custom-call(f32[4,8,2304]{2,1,0:T(8,128)} %refs_0_.1, s32[2,16]{1,0:T(2,128)} %refs_1_.1, bf16[16,128]{1,0:T(8,128)(2,1)} %constant.14.clone.refs_2_, f32[8,1024]{1,0:T(8,128)} %constant.15.clone.refs_3_, s32[4,64]{1,0:T(4,128)} %bitcast.3, s32[4,64]{1,0:T(4,128)} %bitcast.4, ...), custom_call_target="tpu_custom_call" | custom-call | tf_op jit(solution)/shard_map/section/pallas_call | solution.py:577
  34.9 2.1 %finish.1 = f32[4,8,2304]{2,1,0:T(8,128)} custom-call(f32[4,8,2304]{2,1,0:T(8,128)} %get-tuple-element.7.base, f32[192,128]{1,0:T(8,128)} %get-tuple-element.8.outer), custom_call_target="tpu_custom_call" | custom-call | tf_op jit(solution)/shard_map/finish/pallas_call | solution.py:588

commit v9 on v7

--- a/solution.py
+++ b/solution.py
@@ -211,9 +211,6 @@
     state_tiles = elems * NODES // LANES
 
     loads = [pltpu.make_async_copy(a, b, load_sems.at[i]) for i, (a, b) in enumerate(zip(given, held))]
-    for load in loads[:4]:
-        load.start()
-
     barrier = pltpu.get_barrier_semaphore()
 
     def greet(k, carry):
@@ -224,7 +221,7 @@
 
     pl.semaphore_signal(barrier, 1, device_id=(lower, me), device_id_type=MESH)
     lax.fori_loop(1, span, greet, 0)
-    for load in loads[4:]:
+    for load in loads:
         load.start()
 
     lane = lax.broadcasted_iota(jnp.int32, (8, LANES), 1)

time: 37.1 us -> 37.1 us (level)
  no operation moved by 1% of the time
where the time goes in v9:
time: 37.1 us; the launch traced here: 36.9 us
  Pallas kernels  36.9 us (99%)
    pallas_call x1, Pallas kernels, body(): pl.pallas_call(functools.partial(kernel, groups, span), out_shape=(whole,...  34.9 us
    pallas_call x1, Pallas kernels, body(): pl.pallas_call(functools.partial(finish, span), out_shape=whole, in_specs...  1.99 us

profile of v9, /device:TPU:1, one launch (start us, length us, event | category | flops | bytes accessed | tf_op | source)
XLA Modules:
  0.0 36.9 jit_solution(10576023897415968118)
XLA Ops:
  0.0 34.9 %section.1 = (f32[4,8,2304]{2,1,0:T(8,128)}, f32[192,128]{1,0:T(8,128)}) custom-call(f32[4,8,2304]{2,1,0:T(8,128)} %refs_0_.1, s32[2,16]{1,0:T(2,128)} %refs_1_.1, bf16[16,128]{1,0:T(8,128)(2,1)} %constant.14.clone.refs_2_, f32[8,1024]{1,0:T(8,128)} %constant.15.clone.refs_3_, s32[4,64]{1,0:T(4,128)} %bitcast.3, s32[4,64]{1,0:T(4,128)} %bitcast.4, ...), custom_call_target="tpu_custom_call" | custom-call | tf_op jit(solution)/shard_map/section/pallas_call | solution.py:574
  34.9 2.0 %finish.1 = f32[4,8,2304]{2,1,0:T(8,128)} custom-call(f32[4,8,2304]{2,1,0:T(8,128)} %get-tuple-element.7.base, f32[192,128]{1,0:T(8,128)} %get-tuple-element.8.outer), custom_call_target="tpu_custom_call" | custom-call | tf_op jit(solution)/shard_map/finish/pallas_call | solution.py:585
